TPU v7x, 32 devices: a whole 2x2x4 slice. The times are simulated.
32 devices in a mesh: dp: 8 (over z, y), mp: 4 (over x, core).
Axes of the slice: x: 2, y: 2, z: 4, core: 2. Of those that a mesh axis runs over, the one named last changes fastest.
Arguments:
- x_in: bfloat16 [16384, 1024], P(('dp', 'mp')), may hold values from -6 to 6
- out_grad: bfloat16 [16384, 1024], P(('dp', 'mp')), may hold values from -6 to 6
- item_lengths: int32 [16, 8], P('dp'), may hold values from 0 to 512, as said below
- weight_store: float32 [4, 384, 128, 64], P('mp', 'dp'), may hold values from -2 to 2
- owner_perm: int32 [4, 384], P('mp'), may hold values from 0 to 383, as said below
- left_roots: float32 [4, 384, 128, 128], P('mp', 'dp'), may hold values from -8 to 24
- right_roots: float32 [4, 384, 64, 64], P('mp', 'dp'), may hold values from -8 to 24
- left_stats: float32 [4, 384, 128, 128], P('mp', 'dp'), may hold values from -2048 to 2048
- right_stats: float32 [4, 384, 64, 64], P('mp', 'dp'), may hold values from -2048 to 2048
- head_vectors: float32 [4, 512], P('mp', 'dp'), may hold values from -3 to 3
- head_first: float32 [4, 512], P('mp', 'dp'), may hold values from -98304 to 98304
- head_second: float32 [4, 512], P('mp', 'dp'), may hold values from 327 to 3276
- shared_vectors: float32 [10240], P(('dp', 'mp')), may hold values from -1 to 2
- shared_first: float32 [10240], P(('dp', 'mp')), may hold values from -98304 to 98304
- shared_second: float32 [10240], P(('dp', 'mp')), may hold values from 0 to 163
Outputs:
- layer_out: bfloat16 [16384, 1024], P(('dp', 'mp'))
- input_grad: float32 [16384, 1024], P(('dp', 'mp'))
- block_grads: float32 [4, 384, 128, 64], P('mp', 'dp')
- new_left: float32 [4, 384, 128, 128], P('mp', 'dp')
- new_right: float32 [4, 384, 64, 64], P('mp', 'dp')
- new_weights: float32 [4, 384, 128, 64], P('mp', 'dp')
- new_head_first: float32 [4, 512], P('mp', 'dp')
- new_head_second: float32 [4, 512], P('mp', 'dp')
- new_head: float32 [4, 512], P('mp', 'dp')
- new_shared_first: float32 [10240], P(('dp', 'mp'))
- new_shared_second: float32 [10240], P(('dp', 'mp'))
- new_shared: float32 [10240], P(('dp', 'mp'))
Inputs may be any that keep to these rules, and one draw needn't show every extreme that they name: `item_lengths`: each row lists its items' lengths, each 128 or 512, in any order, then zeros; a row's lengths sum to 1024. `owner_perm`: each row is a permutation of the 384 blocks of that index's panel.
All inputs are finite; a program needn't handle non-finite values.
Results may differ from a plain program's by a relative error of at most 0.017.
Values may be sent and summed in bfloat16 or wider, within the bound.
No kernel may reach another device: no remote copies, remote signals or barrier semaphores. Data moves between devices by JAX's collectives and lax.ppermute only.
A program may use at most 256 MiB of HBM per device.

v0:
```python
from functools import partial

import jax
import jax.numpy as jnp
from jax import lax
from jax.sharding import PartitionSpec as P

DH = 64
SLOTS = 1024
STEP = 10


def normalize_keep(inputs, gain, shift):
    center = inputs - jnp.mean(inputs, axis=-1, keepdims=True)
    spread = jnp.mean(center * center, axis=-1, keepdims=True)
    inverse = lax.rsqrt(spread + 1e-05)
    scaled = center * inverse
    return (scaled * gain + shift, scaled, inverse)


def normalize_back(upstream, scaled, inverse, gain):
    gained = upstream * gain
    result = inverse * (
        gained
        - jnp.mean(gained, axis=-1, keepdims=True)
        - scaled * jnp.mean(gained * scaled, axis=-1, keepdims=True)
    )
    return (result, jnp.sum(upstream * scaled, axis=0), jnp.sum(upstream, axis=0))


def over_rows(left_side, right_side):
    return lax.dot_general(
        left_side, right_side, (((0,), (0,)), ((), ())), preferred_element_type=jnp.float32
    )


def over_cols(left_side, right_side):
    return lax.dot_general(
        left_side, right_side, (((1,), (1,)), ((), ())), preferred_element_type=jnp.float32
    )


def row_slice(matrix, width_of):
    return lax.slice_in_dim(matrix, 0, width_of, axis=0)


def masked_scores(query_row, key_row, segment):
    scores = jnp.einsum(
        "qhd,khd->hqk", query_row, key_row, preferred_element_type=jnp.float32
    ) * DH ** (-0.5)
    same_item = segment[:, None] == segment[None, :]
    return jnp.where(same_item[None], scores, -1e30)


def attend_forward(packed):
    query_row, key_row, value_row, segment = packed
    masked = masked_scores(query_row, key_row, segment)
    maximum = jnp.max(masked, axis=-1, keepdims=True)
    exponent = jnp.exp(masked - maximum)
    totals = jnp.sum(exponent, axis=-1, keepdims=True)
    attention = (exponent / totals).astype(jnp.bfloat16)
    context = jnp.einsum("hqk,khd->qhd", attention, value_row, preferred_element_type=jnp.float32)
    return (context.astype(jnp.bfloat16), maximum + jnp.log(totals))


def attend_backward(packed):
    query_row, key_row, value_row, segment, context_grad, log_total = packed
    masked = masked_scores(query_row, key_row, segment)
    attention = jnp.exp(masked - log_total)
    weight_grad = jnp.einsum(
        "qhd,khd->hqk", context_grad, value_row, preferred_element_type=jnp.float32
    )
    value_grad = jnp.einsum(
        "hqk,qhd->khd",
        attention.astype(jnp.bfloat16),
        context_grad,
        preferred_element_type=jnp.float32,
    )
    centre = jnp.sum(attention * weight_grad, axis=-1, keepdims=True)
    score_grad = (attention * (weight_grad - centre)).astype(jnp.bfloat16)
    scaling = DH ** (-0.5)
    query_grad = (
        jnp.einsum("hqk,khd->qhd", score_grad, key_row, preferred_element_type=jnp.float32)
        * scaling
    )
    key_grad = (
        jnp.einsum("hqk,qhd->khd", score_grad, query_row, preferred_element_type=jnp.float32)
        * scaling
    )
    return (
        query_grad.astype(jnp.bfloat16),
        key_grad.astype(jnp.bfloat16),
        value_grad.astype(jnp.bfloat16),
    )


def adam_update(current, moment_one, moment_two, gradient):
    first_new = 0.9 * moment_one + 0.1 * gradient
    second_new = 0.999 * moment_two + 0.001 * gradient * gradient
    stepped = first_new / (1.0 - 0.9**STEP) / (jnp.sqrt(second_new / (1.0 - 0.999**STEP)) + 1e-08)
    return (first_new, second_new, current - 0.3 * stepped)


def shards(
    x_in,
    out_grad,
    item_lengths,
    weight_store,
    owner_perm,
    left_roots,
    right_roots,
    left_stats,
    right_stats,
    head_vectors,
    head_first,
    head_second,
    shared_vectors,
    shared_first,
    shared_second,
):
    model_ways = lax.axis_size("mp")
    batch_ways = lax.axis_size("dp")
    model_width = x_in.shape[1]
    shard_rows = x_in.shape[0]
    token_rows = shard_rows * model_ways
    gathered_blocks, gathered_heads = (
        lax.all_gather(weight_store, "dp", axis=1, tiled=True),
        lax.all_gather(head_vectors, "dp", axis=1, tiled=True),
    )
    shared = lax.all_gather(shared_vectors, ("dp", "mp"), axis=0, tiled=True)
    perm_row = owner_perm[0]
    block_count = perm_row.shape[0]
    indices = jnp.arange(block_count, dtype=jnp.int32)
    inverse = jnp.sum(jnp.where(perm_row[:, None] == indices[None, :], indices[:, None], 0), axis=0)
    natural = gathered_blocks[0][inverse]
    row_block = natural.shape[1]
    col_block = natural.shape[2]
    row_groups = model_width // row_block
    col_groups = block_count // row_groups
    weight_panel = natural.reshape(col_groups, row_groups, row_block, col_block).transpose(
        1, 2, 0, 3
    )
    weight_panel = weight_panel.reshape(model_width, col_groups * col_block).astype(jnp.bfloat16)
    head_width = model_width // model_ways
    ffn_width = (col_groups * col_block - 4 * head_width) // 2
    qkv_weights = weight_panel[:, : 3 * head_width]
    out_weight = weight_panel[:, 3 * head_width : 4 * head_width]
    w_one_local = weight_panel[:, 4 * head_width : 4 * head_width + ffn_width]
    w_two_local = weight_panel[:, 4 * head_width + ffn_width :]
    head_values = gathered_heads[0]
    bias_query = head_values[:head_width]
    bias_value = head_values[head_width:]
    bias_output = shared[0:model_width]
    bias_outer = shared[model_width : 2 * model_width]
    gain_one = shared[2 * model_width : 3 * model_width]
    shift_one = shared[3 * model_width : 4 * model_width]
    gain_two = shared[4 * model_width : 5 * model_width]
    shift_two = shared[5 * model_width : 6 * model_width]
    bias_inner = shared[6 * model_width :]
    ffn_total = bias_inner.shape[0]
    bounds = jnp.cumsum(item_lengths, axis=1)
    position = jnp.arange(SLOTS, dtype=jnp.int32)
    segments = jnp.sum((position[None, :, None] >= bounds[:, None, :]).astype(jnp.int32), axis=2)
    inputs_all = lax.all_gather(x_in, "mp", axis=0, tiled=True)
    projected = jnp.dot(inputs_all, qkv_weights, preferred_element_type=jnp.float32)
    row_count = token_rows // SLOTS
    head_shape = (row_count, SLOTS, head_width // DH, DH)
    query_heads = (projected[:, :head_width] + bias_query).astype(jnp.bfloat16).reshape(head_shape)
    key_heads = projected[:, head_width : 2 * head_width].astype(jnp.bfloat16).reshape(head_shape)
    value_heads = (
        (projected[:, 2 * head_width :] + bias_value).astype(jnp.bfloat16).reshape(head_shape)
    )
    context, log_total = lax.map(attend_forward, (query_heads, key_heads, value_heads, segments))
    context_flat = context.reshape(token_rows, head_width)
    attended = lax.psum_scatter(
        over_cols(row_slice(context_flat, lax.axis_size("mp") * shard_rows), out_weight),
        "mp",
        scatter_dimension=0,
        tiled=True,
    )
    hidden = x_in.astype(jnp.float32) + attended + bias_output
    middle, middle_scaled, middle_inverse = normalize_keep(hidden, gain_one, shift_one)
    middle_low = middle.astype(jnp.bfloat16)
    gelu_exact = partial(jax.nn.gelu, approximate=False)
    middle_all = lax.all_gather(middle_low, "mp", axis=0, tiled=True)
    column_start = lax.axis_index("mp") * ffn_width
    bias_local = lax.dynamic_slice_in_dim(bias_inner, column_start, ffn_width, 0)
    activated, gelu_pull = jax.vjp(
        gelu_exact,
        jnp.dot(middle_all, w_one_local, preferred_element_type=jnp.float32) + bias_local,
    )
    activated_low = activated.astype(jnp.bfloat16)
    ffn_result = lax.psum_scatter(
        over_cols(row_slice(activated_low, lax.axis_size("mp") * shard_rows), w_two_local).astype(
            jnp.bfloat16
        ),
        "mp",
        scatter_dimension=0,
        tiled=True,
    ).astype(jnp.float32)
    outer_sum = middle + ffn_result + bias_outer
    layer_value, out_scaled, out_inverse = normalize_keep(outer_sum, gain_two, shift_two)
    resid_grad, grad_gain_two, grad_shift_two = normalize_back(
        out_grad.astype(jnp.float32), out_scaled, out_inverse, gain_two
    )
    grad_bias_outer = jnp.sum(resid_grad, axis=0)
    resid_low = resid_grad.astype(jnp.bfloat16)
    resid_all = lax.all_gather(resid_low, "mp", axis=0, tiled=True)
    before_grad = gelu_pull(jnp.dot(resid_all, w_two_local, preferred_element_type=jnp.float32))[
        0
    ].astype(jnp.bfloat16)
    grad_w_one = over_rows(middle_all, before_grad)
    grad_w_two = over_rows(resid_all, activated_low)
    grad_bias_inner = lax.dynamic_update_slice_in_dim(
        jnp.zeros((ffn_total,), jnp.float32),
        jnp.sum(before_grad.astype(jnp.float32), axis=0),
        column_start,
        0,
    )
    middle_grad = resid_grad + lax.psum_scatter(
        over_cols(row_slice(before_grad, lax.axis_size("mp") * shard_rows), w_one_local).astype(
            jnp.bfloat16
        ),
        "mp",
        scatter_dimension=0,
        tiled=True,
    ).astype(jnp.float32)
    hidden_grad, grad_gain_one, grad_shift_one = normalize_back(
        middle_grad, middle_scaled, middle_inverse, gain_one
    )
    grad_bias_output = jnp.sum(hidden_grad, axis=0)
    hidden_all = lax.all_gather(hidden_grad.astype(jnp.bfloat16), "mp", axis=0, tiled=True)
    grad_out_weight = over_rows(hidden_all, context_flat)
    context_grad = (
        jnp.dot(hidden_all, out_weight, preferred_element_type=jnp.float32)
        .astype(jnp.bfloat16)
        .reshape(head_shape)
    )
    query_grad, key_grad, value_grad = lax.map(
        attend_backward, (query_heads, key_heads, value_heads, segments, context_grad, log_total)
    )
    qkv_grad = jnp.concatenate(
        [
            query_grad.reshape(token_rows, head_width),
            key_grad.reshape(token_rows, head_width),
            value_grad.reshape(token_rows, head_width),
        ],
        axis=1,
    )
    grad_qkv = over_rows(inputs_all, qkv_grad)
    input_grad = hidden_grad + lax.psum_scatter(
        over_cols(row_slice(qkv_grad, lax.axis_size("mp") * shard_rows), qkv_weights).astype(
            jnp.bfloat16
        ),
        "mp",
        scatter_dimension=0,
        tiled=True,
    ).astype(jnp.float32)
    column_sums = jnp.sum(qkv_grad.astype(jnp.float32), axis=0)
    head_grad = jnp.concatenate([column_sums[:head_width], column_sums[2 * head_width :]])
    grad_panel = jnp.concatenate([grad_qkv, grad_out_weight, grad_w_one, grad_w_two], axis=1)
    grad_natural = grad_panel.reshape(row_groups, row_block, col_groups, col_block).transpose(
        2, 0, 1, 3
    )
    grad_owned = grad_natural.reshape(block_count, row_block, col_block)[perm_row]
    block_grads, head_grad_mine = (
        lax.psum_scatter(
            grad_owned.astype(jnp.bfloat16), "dp", scatter_dimension=0, tiled=True
        ).astype(jnp.float32),
        lax.psum_scatter(
            head_grad.astype(jnp.bfloat16), "dp", scatter_dimension=0, tiled=True
        ).astype(jnp.float32),
    )
    shared_grad_all = jnp.concatenate(
        [
            grad_bias_output,
            grad_bias_outer,
            grad_gain_one,
            grad_shift_one,
            grad_gain_two,
            grad_shift_two,
            grad_bias_inner,
        ]
    )
    shared_grad = lax.psum_scatter(shared_grad_all, ("dp", "mp"), scatter_dimension=0, tiled=True)
    precise = lax.Precision.HIGHEST
    weights_here = weight_store[0]
    token_total = token_rows * batch_ways
    scaled_grads = block_grads * token_total ** (-0.5)
    new_left = 0.5 * left_stats[0] + 0.5 * jnp.einsum(
        "bij,bkj->bik", scaled_grads, scaled_grads, precision=precise
    )
    new_right = 0.5 * right_stats[0] + 0.5 * jnp.einsum(
        "bji,bjk->bik", scaled_grads, scaled_grads, precision=precise
    )
    direction = jnp.einsum("bij,bjk->bik", left_roots[0], block_grads, precision=precise)
    direction = jnp.einsum("bij,bjk->bik", direction, right_roots[0], precision=precise)
    weight_size = jnp.sqrt(
        jnp.mean(weights_here * weights_here, axis=(1, 2), keepdims=True) + 1e-06
    )
    step_size = jnp.sqrt(jnp.mean(direction * direction, axis=(1, 2), keepdims=True) + 1e-06)
    new_weights = weights_here - 0.3 * weight_size * direction / step_size
    head_one, head_two, head_new = adam_update(
        head_vectors[0], head_first[0], head_second[0], head_grad_mine
    )
    shared_one, shared_two, shared_new = adam_update(
        shared_vectors, shared_first, shared_second, shared_grad
    )
    return (
        layer_value.astype(jnp.bfloat16),
        input_grad,
        block_grads[None],
        new_left[None],
        new_right[None],
        new_weights[None],
        head_one[None],
        head_two[None],
        head_new[None],
        shared_one,
        shared_two,
        shared_new,
    )


def solution(mesh):
    placed = (
        P(("dp", "mp"), None),
        P(("dp", "mp"), None),
        P("dp", None),
        P("mp", "dp", None, None),
        P("mp", None),
        P("mp", "dp", None, None),
        P("mp", "dp", None, None),
        P("mp", "dp", None, None),
        P("mp", "dp", None, None),
        P("mp", "dp"),
        P("mp", "dp"),
        P("mp", "dp"),
        P(("dp", "mp")),
        P(("dp", "mp")),
        P(("dp", "mp")),
    )
    return jax.shard_map(
        shards,
        mesh=mesh,
        in_specs=placed,
        out_specs=(
            P(("dp", "mp"), None),
            P(("dp", "mp"), None),
            P("mp", "dp", None, None),
            P("mp", "dp", None, None),
            P("mp", "dp", None, None),
            P("mp", "dp", None, None),
            P("mp", "dp"),
            P("mp", "dp"),
            P("mp", "dp"),
            P(("dp", "mp")),
            P(("dp", "mp")),
            P(("dp", "mp")),
        ),
        check_vma=False,
    )
```

profile of v0, /device:TPU:0, one launch (start us, length us, event | category | flops | bytes accessed | tf_op | source)
XLA Modules:
  0.0 891.5 jit_solution(11781383154895267056)
XLA Ops:
  12.5 23.6 %all-reduce = f32[512]{0:T(512)S(1)} all-reduce(f32[512]{0:T(512)S(1)} %bitcast_dynamic-update-slice_fusion.1), channel_id=1, replica_groups=mesh['dp'=8,'mp'=4] {'dp'}, use_global_device_ids=true, to_apply=%add | all-reduce | flops 512 | bytes 4096
  36.2 76.5 %all-gather.6.cloned.1.call-done = bf16[1,384,128,64]{2,3,0,1:T(8,128)(2,1)} async-done(((bf16[1,48,128,64]{2,3,0,1:T(8,128)(2,1)}), bf16[1,384,128,64]{2,3,0,1:T(8,128)(2,1)}) %all-gather.6.cloned.1.call-update) | async-done | bytes 6291472 | tf_op jit(solution)/shard_map/all_gather | solution.py:127
  112.8 6.8 gather_fusion
  119.6 16.4 %copy.83 = bf16[48,8,128,64]{2,1,3,0:T(8,128)(2,1)S(1)} copy(bf16[48,8,128,64]{2,3,1,0:T(8,128)(2,1)} %bitcast.233) | data formatting | bytes 12582912 | tf_op jit(solution)/shard_map/convert_element_type | solution.py:143
  140.2 6.9 all-gather.8.cloned.1.call-done
  171.8 40.0 %while.26 = (s32[]{:T(128)}, bf16[2,1024,4,64]{1,3,2,0:T(8,128)(2,1)}, f32[2,4,1024,1]{2,1,3,0:T(4,128)S(1)}, bf16[2,1024,4,64]{1,3,2,0:T(8,128)(2,1)}, s32[2,10...) while((s32[]{:T(128)}, ...), condition=%wide.region_6.7_spmd, body=%wide.region_3.6_spmd.sunk | while | flops 1125380096 | bytes 69351608 | solution.py:173
  221.9 39.9 %all-reduce.1 = f32[10240]{0:T(1024)S(1)} all-reduce(f32[10240]{0:T(1024)S(1)} %dynamic-update-slice.1), channel_id=1, replica_groups=mesh['dp'=8,'mp'=4] {'dp','mp'}, use_global_device_ids=true, to_apply=%add.1 | all-reduce | flops 10240 | bytes 81920
  261.8 31.8 %reduce-scatter.6.cloned.1.call-done = f32[512,1024]{1,0:T(8,128)} async-done(((f32[2048,1024]{1,0:T(8,128)}), f32[512,1024]{1,0:T(8,128)}) %reduce-scatter.6.cloned.1.call-update) | async-done | bytes 2097168 | tf_op jit(solution)/shard_map/reduce_scatter | solution.py:175
  298.6 34.6 %all-gather.10.cloned.1.call-done = bf16[2048,1024]{1,0:T(8,128)(2,1)} async-done(((bf16[512,1024]{1,0:T(8,128)(2,1)}), bf16[2048,1024]{1,0:T(8,128)(2,1)}) %all-gather.10.cloned.1.call-update) | async-done | bytes 4194320 | tf_op jit(solution)/shard_map/all_gather | solution.py:185
  333.2 25.9 %multiply_convert_fusion.1 = (bf16[2048,1024]{1,0:T(8,128)(2,1)S(1)}, f32[2048,1024]{1,0:T(8,128)}, f32[2048,1024]{1,0:T(8,128)}) fusion(f32[1024]{0:T(1024)S(1)} %dynamic_slice.36, bf16[2048,1024]{1,0:T(8,128)(2,1)} %all-gather.10.cloned.1.call-done, bf16[1024,3072]{0,1:T(8,128)(2,1)} %bitcast.240), kind=kOutput, calls=%fused_computation.69 | convolution fusion | flops 4433379328 | bytes 27267072 | tf_op jit(solution)/shard_map/dot_general | solution.py:190
  361.0 7.6 convolution_convert_fusion.2
  368.7 44.6 %reduce-scatter.8.cloned.1.call-done = bf16[512,1024]{1,0:T(8,128)(2,1)} async-done(((bf16[2048,1024]{1,0:T(8,128)(2,1)}), bf16[512,1024]{1,0:T(8,128)(2,1)}) %reduce-scatter.8.cloned.1.call-update) | async-done | bytes 1048592 | tf_op jit(solution)/shard_map/reduce_scatter | solution.py:193
  421.0 34.6 %all-gather.12.cloned.1.call-done = bf16[2048,1024]{1,0:T(8,128)(2,1)} async-done(((bf16[512,1024]{1,0:T(8,128)(2,1)}), bf16[2048,1024]{1,0:T(8,128)(2,1)}) %all-gather.12.cloned.1.call-update) | async-done | bytes 4194320 | tf_op jit(solution)/shard_map/all_gather | solution.py:208
  455.6 15.3 %convert_reduce_fusion = (f32[1024]{0:T(1024)}, bf16[2048,1024]{1,0:T(8,128)(2,1)S(1)}) fusion(f32[2048,1024]{1,0:T(8,128)} %get-tuple-element.233, bf16[2048,1024]{1,0:T(8,128)(2,1)} %all-gather.12.cloned.1.call-done, bf16[1024,3072]{0,1:T(8,128)(2,1)} %bitcast.242, f32[2048,1024]{1,0:T(8,128)} %get-tuple-element.255, f32[1024]{0:T(1024)S(1)} %dynamic_slice.36), kind=kOutput, calls=%fused_computation.67 | convolution fusion | flops 4330617856 | bytes 27271168 | tf_op jit(solution)/shard_map/dot_general | solution.py:209
  472.8 7.6 convolution_convert_fusion.1
  480.5 44.6 %reduce-scatter.10.cloned.1.call-done = bf16[512,1024]{1,0:T(8,128)(2,1)} async-done(((bf16[2048,1024]{1,0:T(8,128)(2,1)}), bf16[512,1024]{1,0:T(8,128)(2,1)}) %reduce-scatter.10.cloned.1.call-update) | async-done | bytes 1048592 | tf_op jit(solution)/shard_map/reduce_scatter | solution.py:220
  533.4 34.6 %all-gather.14.cloned.1.call-done = bf16[2048,1024]{1,0:T(8,128)(2,1)} async-done(((bf16[512,1024]{1,0:T(8,128)(2,1)}), bf16[2048,1024]{1,0:T(8,128)(2,1)}) %all-gather.14.cloned.1.call-update) | async-done | bytes 4194320 | tf_op jit(solution)/shard_map/all_gather | solution.py:232
  584.4 97.7 %while.27 = (s32[]{:T(128)}, bf16[2,1024,4,64]{1,3,2,0:T(8,128)(2,1)}, bf16[2,1024,4,64]{1,3,2,0:T(8,128)(2,1)}, bf16[2,1024,4,64]{1,3,2,0:T(8,128)(2,1)}, bf16[...) while((s32[]{:T(128)}, ...), condition=%wide.region_20.21_spmd, body=%wide.region_18.20_spmd.sunk | while | flops 2724458496 | bytes 171017616 | solution.py:239
  585.3 9.4 %fusion.167 = f32[4,1024,1024]{1,2,0:T(8,128)} fusion(bf16[2,1024,4,64]{1,3,2,0:T(8,128)(2,1)} %get-tuple-element.429, s32[]{:T(128)S(6)} %copy.133, bf16[2,1024,4,64]{1,3,2,0:T(8,128)(2,1)} %get-tuple-element.428), kind=kOutput, calls=%fused_computation.42.clone.1 | convolution fusion | flops 536870912 | bytes 17826816 | tf_op jit(solution)/shard_map/while/body/eval_jaxpr/qhd,khd->hqk/dot_general | solution.py:70
  594.8 12.7 %multiply_reduce_fusion.8 = (f32[4,1024]{1,0:T(4,128)S(1)}, f32[4,1024,1024]{1,2,0:T(8,128)}) fusion(f32[4,1024,1024]{1,2,0:T(8,128)} %fusion.167, f32[4,1024]{1,0:T(4,128)S(1)} %dynamic-slice_bitcast_fusion.2, bf16[2,1024,4,64]{1,3,2,0:T(8,128)(2,1)S(1)} %copy-done.4, s32[]{:T(128)S(6)} %copy.133, bf16[2,1024,4,64]{1,3,2,0:T(8,128)(2,1)S(1)} %copy-done.3, ...), kind=kOutput, calls=%fused_computation.26.clone.1 | convolution fusion | flops 557838336 | bytes 35685376 | tf_op jit(solution)/shard_map/while/body/eval_jaxpr/qhd,khd->hqk/dot_general | solution.py:48
  607.5 12.0 %multiply_convert_fusion.3 = bf16[4,1024,1024]{1,2,0:T(8,128)(2,1)S(1)} fusion(f32[4,1024,1024]{1,2,0:T(8,128)} %get-tuple-element.372, f32[4,1024,1024]{1,2,0:T(8,128)} %fusion.167, f32[4,1024]{1,0:T(4,128)S(1)} %get-tuple-element.373), kind=kLoop, calls=%fused_computation.25.clone.1 | loop fusion | flops 12582912 | bytes 41959424 | tf_op jit(solution)/shard_map/while/body/eval_jaxpr/convert_element_type | solution.py:80
  619.5 8.5 fusion.170
  634.0 9.4 %fusion.167 = f32[4,1024,1024]{1,2,0:T(8,128)} fusion(bf16[2,1024,4,64]{1,3,2,0:T(8,128)(2,1)} %get-tuple-element.429, s32[]{:T(128)S(6)} %copy.133, bf16[2,1024,4,64]{1,3,2,0:T(8,128)(2,1)} %get-tuple-element.428), kind=kOutput, calls=%fused_computation.42.clone.1 | convolution fusion | flops 536870912 | bytes 17826816 | tf_op jit(solution)/shard_map/while/body/eval_jaxpr/qhd,khd->hqk/dot_general | solution.py:70
  643.4 12.7 %multiply_reduce_fusion.8 = (f32[4,1024]{1,0:T(4,128)S(1)}, f32[4,1024,1024]{1,2,0:T(8,128)}) fusion(f32[4,1024,1024]{1,2,0:T(8,128)} %fusion.167, f32[4,1024]{1,0:T(4,128)S(1)} %dynamic-slice_bitcast_fusion.2, bf16[2,1024,4,64]{1,3,2,0:T(8,128)(2,1)S(1)} %copy-done.4, s32[]{:T(128)S(6)} %copy.133, bf16[2,1024,4,64]{1,3,2,0:T(8,128)(2,1)S(1)} %copy-done.3, ...), kind=kOutput, calls=%fused_computation.26.clone.1 | convolution fusion | flops 557838336 | bytes 35685376 | tf_op jit(solution)/shard_map/while/body/eval_jaxpr/qhd,khd->hqk/dot_general | solution.py:48
  656.1 12.0 %multiply_convert_fusion.3 = bf16[4,1024,1024]{1,2,0:T(8,128)(2,1)S(1)} fusion(f32[4,1024,1024]{1,2,0:T(8,128)} %get-tuple-element.372, f32[4,1024,1024]{1,2,0:T(8,128)} %fusion.167, f32[4,1024]{1,0:T(4,128)S(1)} %get-tuple-element.373), kind=kLoop, calls=%fused_computation.25.clone.1 | loop fusion | flops 12582912 | bytes 41959424 | tf_op jit(solution)/shard_map/while/body/eval_jaxpr/convert_element_type | solution.py:80
  668.2 8.5 fusion.170
  696.8 8.2 fusion.117
  724.8 6.8 gather_fusion.1
  734.7 41.7 %all-reduce.3 = f32[10240]{0:T(1024)S(1)} all-reduce(f32[10240]{0:T(1024)S(1)} %constant_dynamic-update-slice_fusion.4), channel_id=8, replica_groups=mesh['dp'=8,'mp'=4] {'dp','mp'}, use_global_device_ids=true, to_apply=%region_34.35.clone | all-reduce | flops 10240 | bytes 81920
  779.7 22.7 %all-reduce.2 = bf16[512]{0:T(512)(128)(2,1)S(1)} all-reduce(bf16[512]{0:T(512)(128)(2,1)S(1)} %pad_maximum_fusion), channel_id=7, replica_groups=mesh['dp'=8,'mp'=4] {'dp'}, use_global_device_ids=true, to_apply=%region_26.27.clone | all-reduce | flops 512 | bytes 2048
  806.7 56.6 %reduce-scatter.14.cloned.1.call-done = bf16[48,128,64]{1,2,0:T(8,128)(2,1)} async-done(((bf16[384,128,64]{1,2,0:T(8,128)(2,1)}), bf16[48,128,64]{1,2,0:T(8,128)(2,1)}) %reduce-scatter.14.cloned.1.call-update) | async-done | bytes 786448 | tf_op jit(solution)/shard_map/reduce_scatter | solution.py:267
  877.6 6.9 fusion.63
  (272 shorter events, 184.3 us)
Async XLA Ops:
  7.2 856.2 %copy-start = (f32[1,48,128,128]{3,2,1,0:T(8,128)S(1)}, f32[1,48,128,128]{3,2,1,0:T(8,128)}, u32[]{:S(2)}) copy-start(f32[1,48,128,128]{3,2,1,0:T(8,128)} %param.24) | copy-start | bytes 9437188
  7.2 105.5 %all-gather.6.cloned.1.call-start = ((), (), s32[]{:S(2)}) async-start(), calls=%async_computation.5 | async-start | bytes 7077888 | tf_op jit(solution)/shard_map/all_gather | solution.py:127
  9.9 137.1 %all-gather.8.cloned.1.call-start = ((), (), s32[]{:S(2)}) async-start(), calls=%async_computation.6 | async-start | bytes 5242880 | tf_op jit(solution)/shard_map/all_gather | solution.py:164
  10.6 283.0 %reduce-scatter.6.cloned.1.call-start = ((), (), s32[]{:S(2)}) async-start(), calls=%async_computation.7 | async-start | bytes 10485760 | tf_op jit(solution)/shard_map/reduce_scatter | solution.py:175
  221.0 112.1 %all-gather.10.cloned.1.call-start = ((), (), s32[]{:S(2)}) async-start(), calls=%async_computation.8 | async-start | bytes 5242880 | tf_op jit(solution)/shard_map/all_gather | solution.py:185
  298.5 114.8 %reduce-scatter.8.cloned.1.call-start = ((), (), s32[]{:S(2)}) async-start(), calls=%async_computation.9 | async-start | bytes 5242880 | tf_op jit(solution)/shard_map/reduce_scatter | solution.py:193
  368.7 86.9 %all-gather.12.cloned.1.call-start = ((), (), s32[]{:S(2)}) async-start(), calls=%async_computation.10 | async-start | bytes 5242880 | tf_op jit(solution)/shard_map/all_gather | solution.py:208
  420.9 104.2 %reduce-scatter.10.cloned.1.call-start = ((), (), s32[]{:S(2)}) async-start(), calls=%async_computation.11 | async-start | bytes 5242880 | tf_op jit(solution)/shard_map/reduce_scatter | solution.py:220
  480.5 87.5 %all-gather.14.cloned.1.call-start = ((), (), s32[]{:S(2)}) async-start(), calls=%async_computation.12 | async-start | bytes 5242880 | tf_op jit(solution)/shard_map/all_gather | solution.py:232
  533.4 269.7 %reduce-scatter.12.cloned.1.call-start = ((), (), s32[]{:S(2)}) async-start(), calls=%async_computation.13 | async-start | bytes 5242880 | tf_op jit(solution)/shard_map/reduce_scatter | solution.py:251
  585.3 9.5 %copy-start.3 = (bf16[2,1024,4,64]{1,3,2,0:T(8,128)(2,1)S(1)}, bf16[2,1024,4,64]{1,3,2,0:T(8,128)(2,1)}, u32[]{:S(2)}) copy-start(bf16[2,1024,4,64]{1,3,2,0:T(8,128)(2,1)} %get-tuple-element.426) | copy-start | bytes 3145732 | tf_op jit(solution)/shard_map/while
  585.3 9.5 %copy-start.4 = (bf16[2,1024,4,64]{1,3,2,0:T(8,128)(2,1)S(1)}, bf16[2,1024,4,64]{1,3,2,0:T(8,128)(2,1)}, u32[]{:S(2)}) copy-start(bf16[2,1024,4,64]{1,3,2,0:T(8,128)(2,1)} %get-tuple-element.424) | copy-start | bytes 3145732 | tf_op jit(solution)/shard_map/while
  607.4 12.0 %copy-start.5 = (bf16[2,1024,4,64]{1,3,2,0:T(8,128)(2,1)S(1)}, bf16[2,1024,4,64]{1,3,2,0:T(8,128)(2,1)}, u32[]{:S(2)}) copy-start(bf16[2,1024,4,64]{1,3,2,0:T(8,128)(2,1)} %get-tuple-element.428) | copy-start | bytes 3145732 | tf_op jit(solution)/shard_map/while
  607.5 12.0 %copy-start.17 = (bf16[2,1024,4,64]{1,3,2,0:T(8,128)(2,1)S(1)}, bf16[2,1024,4,64]{1,3,2,0:T(8,128)(2,1)}, u32[]{:S(2)}) copy-start(bf16[2,1024,4,64]{1,3,2,0:T(8,128)(2,1)} %get-tuple-element.412) | copy-start | bytes 3145732 | tf_op jit(solution)/shard_map/while
  619.5 8.5 copy-start.19
  634.0 9.5 %copy-start.3 = (bf16[2,1024,4,64]{1,3,2,0:T(8,128)(2,1)S(1)}, bf16[2,1024,4,64]{1,3,2,0:T(8,128)(2,1)}, u32[]{:S(2)}) copy-start(bf16[2,1024,4,64]{1,3,2,0:T(8,128)(2,1)} %get-tuple-element.426) | copy-start | bytes 3145732 | tf_op jit(solution)/shard_map/while
  634.0 9.5 %copy-start.4 = (bf16[2,1024,4,64]{1,3,2,0:T(8,128)(2,1)S(1)}, bf16[2,1024,4,64]{1,3,2,0:T(8,128)(2,1)}, u32[]{:S(2)}) copy-start(bf16[2,1024,4,64]{1,3,2,0:T(8,128)(2,1)} %get-tuple-element.424) | copy-start | bytes 3145732 | tf_op jit(solution)/shard_map/while
  656.1 12.0 %copy-start.5 = (bf16[2,1024,4,64]{1,3,2,0:T(8,128)(2,1)S(1)}, bf16[2,1024,4,64]{1,3,2,0:T(8,128)(2,1)}, u32[]{:S(2)}) copy-start(bf16[2,1024,4,64]{1,3,2,0:T(8,128)(2,1)} %get-tuple-element.428) | copy-start | bytes 3145732 | tf_op jit(solution)/shard_map/while
  656.1 12.0 %copy-start.17 = (bf16[2,1024,4,64]{1,3,2,0:T(8,128)(2,1)S(1)}, bf16[2,1024,4,64]{1,3,2,0:T(8,128)(2,1)}, u32[]{:S(2)}) copy-start(bf16[2,1024,4,64]{1,3,2,0:T(8,128)(2,1)} %get-tuple-element.412) | copy-start | bytes 3145732 | tf_op jit(solution)/shard_map/while
  668.1 8.5 copy-start.19
  696.1 167.2 %reduce-scatter.14.cloned.1.call-start = ((), (), s32[]{:S(2)}) async-start(), calls=%async_computation.14 | async-start | bytes 7077888 | tf_op jit(solution)/shard_map/reduce_scatter | solution.py:267
  696.8 8.2 copy-start.50
  696.8 8.2 copy-start.54
  705.0 5.3 copy-start.14
  705.0 5.3 copy-start.51
  731.7 44.7 %copy-start.37 = (f32[320]{0:T(512)S(1)}, f32[320]{0:T(512)}, u32[]{:S(2)}) copy-start(f32[320]{0:T(512)} %param.31) | copy-start | bytes 3844
  731.7 44.7 %copy-start.42 = (f32[320]{0:T(512)S(1)}, f32[320]{0:T(512)}, u32[]{:S(2)}) copy-start(f32[320]{0:T(512)} %param.33) | copy-start | bytes 3844
  731.7 44.7 %copy-start.43 = (f32[320]{0:T(512)S(1)}, f32[320]{0:T(512)}, u32[]{:S(2)}) copy-start(f32[320]{0:T(512)} %param.32) | copy-start | bytes 3844
  731.7 70.7 %copy-start.46 = (f32[1,64]{1,0:T(1,128)S(1)}, f32[1,64]{1,0:T(1,128)}, u32[]{:S(2)}) copy-start(f32[1,64]{1,0:T(1,128)} %param.28) | copy-start | bytes 772
  731.7 70.7 %copy-start.47 = (f32[1,64]{1,0:T(1,128)S(1)}, f32[1,64]{1,0:T(1,128)}, u32[]{:S(2)}) copy-start(f32[1,64]{1,0:T(1,128)} %param.30) | copy-start | bytes 772
  731.7 70.7 %copy-start.48 = (f32[1,64]{1,0:T(1,128)S(1)}, f32[1,64]{1,0:T(1,128)}, u32[]{:S(2)}) copy-start(f32[1,64]{1,0:T(1,128)} %param.29) | copy-start | bytes 772
  863.3 7.7 copy-start.8
  (45 other events, 125.1 us)
Sparse Core Ops, SparseCore 0:
  10.8 101.8 all-gather.5
  114.3 32.6 all-gather.7
  221.2 72.4 reduce-scatter.5
  298.7 34.4 all-gather.9
  368.8 44.5 reduce-scatter.7
  421.1 34.4 all-gather.11
  480.6 44.4 reduce-scatter.9
  533.5 34.4 all-gather.13
  696.3 44.5 reduce-scatter.11
  744.2 119.0 reduce-scatter.13
where the time goes:
time: 897 us; the launch traced here: 891 us
  waiting for transfers between devices  366 us (41%)
  matrix products  204 us (23%)
  blocking collectives  128 us (14%)
  local copies, waits for them, and re-layouts  95.3 us (11%)
  other arithmetic  70.7 us (8%)
  between operations  16.5 us (2%)
  loops' own time  11.3 us (1%)
    unnamed x4, blocking collectives  128 us
    all_gather x1, waiting for transfers between devices, shards(): lax.all_gather(weight_store, 'dp', axis=1, tiled=True)  76.5 us
    reduce_scatter x1, waiting for transfers between devices, shards(): lax.psum_scatter(grad_owned.astype(jnp.bfloat16), 'dp', scatter_dimension...  56.6 us
    reduce_scatter x1, waiting for transfers between devices, shards(): lax.psum_scatter(over_cols(row_slice(activated_low, lax.axis_size('mp') *...  44.6 us
    reduce_scatter x1, waiting for transfers between devices, shards(): lax.psum_scatter(over_cols(row_slice(before_grad, lax.axis_size('mp') * s...  44.6 us
    all_gather x1, waiting for transfers between devices, shards(): resid_all = lax.all_gather(resid_low, 'mp', axis=0, tiled=True)  34.6 us
    all_gather x1, waiting for transfers between devices, shards(): lax.all_gather(hidden_grad.astype(jnp.bfloat16), 'mp', axis=0, tiled=True)  34.6 us
    all_gather x1, waiting for transfers between devices, shards(): middle_all = lax.all_gather(middle_low, 'mp', axis=0, tiled=True)  34.6 us
  transfers between devices with their start and end apart: 10, of which 9 were waited for; matrix products, arithmetic and copies ran while one was open for 8% of the time, Pallas kernels for 0%

commit v1 on v0

v1 whole, which is shorter than its diff:
```python
from functools import partial

import jax
import jax.numpy as jnp
from jax import lax
from jax.experimental import pallas as pl
from jax.experimental.pallas import tpu as pltpu
from jax.sharding import PartitionSpec as P

DH = 64
SLOTS = 1024
STEP = 10
SHORT = 128
LONG = 512
EXTRA = 16
LOW = jnp.bfloat16
BOTH = ("dp", "mp")
ANY = pl.BlockSpec(memory_space=pl.ANY)
VMEM = pl.BlockSpec(memory_space=pltpu.VMEM)


def normalize_keep(inputs, gain, shift):
    center = inputs - jnp.mean(inputs, axis=-1, keepdims=True)
    spread = jnp.mean(center * center, axis=-1, keepdims=True)
    inverse = lax.rsqrt(spread + 1e-05)
    scaled = center * inverse
    return (scaled * gain + shift, scaled, inverse)


def normalize_back(upstream, scaled, inverse, gain):
    gained = upstream * gain
    result = inverse * (
        gained
        - jnp.mean(gained, axis=-1, keepdims=True)
        - scaled * jnp.mean(gained * scaled, axis=-1, keepdims=True)
    )
    return (result, jnp.sum(upstream * scaled, axis=0), jnp.sum(upstream, axis=0))


def product(left, right, left_dim, right_dim):
    return lax.dot_general(
        left, right, (((left_dim,), (right_dim,)), ((), ())), preferred_element_type=jnp.float32
    )


def adam_update(current, moment_one, moment_two, gradient):
    first_new = 0.9 * moment_one + 0.1 * gradient
    second_new = 0.999 * moment_two + 0.001 * gradient * gradient
    stepped = first_new / (1.0 - 0.9**STEP) / (jnp.sqrt(second_new / (1.0 - 0.999**STEP)) + 1e-08)
    return (first_new, second_new, current - 0.3 * stepped)


def gelu_pair(before):
    below = 0.5 + 0.5 * lax.erf(before * 0.5**0.5)
    slope = below + before * jnp.exp(before * before * -0.5) * 0.3989422804014327
    return before * below, slope


def attend_kernel(start_ref, length_ref, qkv_ref, ctx_ref, lse_ref):
    def item(begin, size):
        width = min(size, 256)
        keys = qkv_ref[1, :, pl.ds(begin, size)]
        values = qkv_ref[2, :, pl.ds(begin, size)]
        for at in range(0, size, width):
            here = pl.ds(begin + at, width)
            scores = product(keys, qkv_ref[0, :, here], 0, 0)
            top = jnp.max(scores, axis=0, keepdims=True)
            expo = jnp.exp(scores - top)
            total = jnp.sum(expo, axis=0, keepdims=True)
            ctx = product(values, expo.astype(LOW), 1, 0) / total
            ctx_ref[:, here] = ctx.astype(LOW)
            lse_ref[0, :, here] = top + jnp.log(total)

    each_item(start_ref, length_ref, item)


def each_item(start_ref, length_ref, item):
    @pl.loop(0, start_ref.shape[0])
    def _(i):
        begin = pl.multiple_of(start_ref[i], SHORT)

        @pl.when(length_ref[i] == LONG)
        def _():
            item(begin, LONG)

        @pl.when(length_ref[i] == SHORT)
        def _():
            item(begin, SHORT)


def attend_back_kernel(start_ref, length_ref, qkv_ref, ctx_ref, dctx_ref, lse_ref, out_ref):
    def item(begin, size):
        width = min(size, 256)
        keys = qkv_ref[1, :, pl.ds(begin, size)]
        values = qkv_ref[2, :, pl.ds(begin, size)]
        dkeys = jnp.zeros((DH, size), jnp.float32)
        dvalues = jnp.zeros((DH, size), jnp.float32)
        for at in range(0, size, width):
            here = pl.ds(begin + at, width)
            queries = qkv_ref[0, :, here]
            dctx = dctx_ref[:, here]
            probs = jnp.exp(product(keys, queries, 0, 0) - lse_ref[0, :, here])
            dprobs = product(values, dctx, 0, 0)
            delta = jnp.sum(
                dctx.astype(jnp.float32) * ctx_ref[:, here].astype(jnp.float32),
                axis=0,
                keepdims=True,
            )
            dscores = (probs * (dprobs - delta)).astype(LOW)
            out_ref[0, :, here] = (product(keys, dscores, 1, 0) * DH**-0.5).astype(LOW)
            dkeys += product(queries, dscores, 1, 1)
            dvalues += product(dctx, probs.astype(LOW), 1, 1)
        out_ref[1, :, pl.ds(begin, size)] = dkeys.astype(LOW)
        out_ref[2, :, pl.ds(begin, size)] = dvalues.astype(LOW)

    each_item(start_ref, length_ref, item)


def attend(starts, lengths, qkv):
    heads = qkv.shape[1] // DH
    return pl.pallas_call(
        attend_kernel,
        out_shape=(
            jax.ShapeDtypeStruct(qkv.shape[1:], LOW),
            jax.ShapeDtypeStruct((heads, 1, SLOTS), jnp.float32),
        ),
        grid_spec=pltpu.PrefetchScalarGridSpec(
            num_scalar_prefetch=2,
            grid=(heads,),
            in_specs=[pl.BlockSpec((3, DH, SLOTS), lambda h, *_: (0, h, 0))],
            out_specs=(
                pl.BlockSpec((DH, SLOTS), lambda h, *_: (h, 0)),
                pl.BlockSpec((1, 1, SLOTS), lambda h, *_: (h, 0, 0)),
            ),
        ),
        compiler_params=pltpu.CompilerParams(vmem_limit_bytes=32 * 2**20),
        cost_estimate=pl.CostEstimate(
            flops=heads * SLOTS * LONG * 1024, bytes_accessed=2**22, transcendentals=heads * 2**19
        ),
    )(starts, lengths, qkv)


def attend_back(starts, lengths, qkv, ctx, dctx, lse):
    heads = qkv.shape[1] // DH
    one = pl.BlockSpec((DH, SLOTS), lambda h, *_: (h, 0))
    three = pl.BlockSpec((3, DH, SLOTS), lambda h, *_: (0, h, 0))
    return pl.pallas_call(
        attend_back_kernel,
        out_shape=jax.ShapeDtypeStruct(qkv.shape, LOW),
        grid_spec=pltpu.PrefetchScalarGridSpec(
            num_scalar_prefetch=2,
            grid=(heads,),
            in_specs=[three, one, one, pl.BlockSpec((1, 1, SLOTS), lambda h, *_: (h, 0, 0))],
            out_specs=three,
        ),
        compiler_params=pltpu.CompilerParams(vmem_limit_bytes=32 * 2**20),
        cost_estimate=pl.CostEstimate(
            flops=heads * SLOTS * LONG * 2560, bytes_accessed=2**23, transcendentals=heads * 2**19
        ),
    )(starts, lengths, qkv, ctx, dctx, lse)


def tile_at(ref, place, groups):
    row = pl.multiple_of(lax.div(place, groups) * DH, DH)
    col = pl.multiple_of(lax.rem(place, groups) * 128, 128)
    return ref.at[pl.ds(row, DH), pl.ds(col, 128)]


def place_kernel(pieces, count, groups, chained, table_ref, *refs):
    sources = refs[:count]
    out_ref, sems = refs[count + chained], refs[count + chained + 1]
    for source, sem, parts in zip(sources, range(count), pieces):
        for row, entry, first, blocks in parts:

            @pl.loop(0, blocks)
            def _(j):
                pltpu.make_async_copy(
                    source.at[pl.ds(pl.multiple_of(row + j * DH, 16), DH), :],
                    tile_at(out_ref, table_ref[entry, first + j], groups),
                    sems.at[sem],
                ).start()

    for source, sem, parts in zip(sources, range(count), pieces):
        total = sum(part[3] for part in parts) * DH
        fits = total <= out_ref.shape[0]
        landed = out_ref.at[pl.ds(0, total), pl.ds(0, 128)] if fits else out_ref
        pltpu.make_async_copy(landed, landed, sems.at[sem]).wait()


def place(table, sources, pieces, shape, previous=None):
    chained = previous is not None
    operands = list(sources) + ([previous] if chained else [])
    return pl.pallas_call(
        partial(place_kernel, pieces, len(sources), shape[1] // 128, int(chained)),
        out_shape=jax.ShapeDtypeStruct(shape, LOW),
        grid_spec=pltpu.PrefetchScalarGridSpec(
            num_scalar_prefetch=1,
            grid=(),
            in_specs=[VMEM] * len(sources) + [ANY] * int(chained),
            out_specs=ANY,
            scratch_shapes=[pltpu.SemaphoreType.DMA((len(sources),))],
        ),
        compiler_params=pltpu.CompilerParams(vmem_limit_bytes=32 * 2**20),
        input_output_aliases={len(operands): 0} if chained else {},
    )(table, *operands)


def fetch_kernel(pieces, groups, table_ref, grad_ref, extra_ref, *refs):
    outs, sems = refs[: len(pieces)], refs[len(pieces)]
    for out, sem, parts in zip(outs, range(len(pieces)), pieces):
        for row, entry, first, blocks in parts:
            if blocks == 0:
                pltpu.make_async_copy(
                    extra_ref.at[entry], out.at[pl.ds(row, EXTRA), :], sems.at[sem]
                ).start()
                continue

            @pl.loop(0, blocks)
            def _(j):
                pltpu.make_async_copy(
                    tile_at(grad_ref, table_ref[entry, first + j], groups),
                    out.at[pl.ds(pl.multiple_of(row + j * DH, 16), DH), :],
                    sems.at[sem],
                ).start()

    for out, sem in zip(outs, range(len(pieces))):
        pltpu.make_async_copy(out, out, sems.at[sem]).wait()


def fetch(table, grad, extra, pieces):
    rows = [sum(part[3] * DH or EXTRA for part in parts) for parts in pieces]
    return pl.pallas_call(
        partial(fetch_kernel, pieces, grad.shape[1] // 128),
        out_shape=tuple(jax.ShapeDtypeStruct((n, 128), LOW) for n in rows),
        grid_spec=pltpu.PrefetchScalarGridSpec(
            num_scalar_prefetch=1,
            grid=(),
            in_specs=[ANY] * 2,
            out_specs=(VMEM,) * len(pieces),
            scratch_shapes=[pltpu.SemaphoreType.DMA((len(pieces),))],
        ),
        compiler_params=pltpu.CompilerParams(vmem_limit_bytes=32 * 2**20),
    )(table, grad, extra)


class Fabric:
    def __init__(self, sizes, row_ways):
        self.batch, self.model = sizes
        self.ways = row_ways
        self.panels = self.model // row_ways
        self.wide = row_ways == 2 and self.panels == 2 and self.batch % 2 == 0
        self.row_groups = [
            list(range(i, i + row_ways)) for i in range(0, self.model, row_ways)
        ]
        self.same_groups = [list(range(t, self.model, row_ways)) for t in range(row_ways)]

    def send(self, value, move):
        pairs = []
        for d in range(self.batch):
            for m in range(self.model):
                e, n = move(d, m)
                pairs.append((d * self.model + m, (e % self.batch) * self.model + n))
        return lax.ppermute(value, BOTH, pairs)

    def to_core(self, value):
        return self.send(value, lambda d, m: (d, m ^ 1))

    def to_x(self, value):
        return self.send(value, lambda d, m: (d, m ^ 2))

    def to_y(self, value):
        return self.send(value, lambda d, m: (d ^ 1, m))

    def to_z(self, value):
        return self.send(value, lambda d, m: (d + 2, m))

    def row_gather(self, own):
        if self.wide:
            other = self.to_core(own)
            first = lax.rem(lax.axis_index("mp"), 2) == 0
            return jnp.concatenate(
                [jnp.where(first, own, other), jnp.where(first, other, own)], axis=0
            )
        return lax.all_gather(own, "mp", axis=0, tiled=True, axis_index_groups=self.row_groups)

    def row_scatter(self, whole):
        rows = whole.shape[0] // self.ways
        if self.wide:
            core = lax.rem(lax.axis_index("mp"), 2)
            mine = lax.dynamic_slice_in_dim(whole, core * rows, rows, 0)
            theirs = lax.dynamic_slice_in_dim(whole, (1 - core) * rows, rows, 0)
            return mine.astype(jnp.float32) + self.to_core(theirs.astype(LOW)).astype(jnp.float32)
        return lax.psum_scatter(
            whole.astype(LOW),
            "mp",
            scatter_dimension=0,
            tiled=True,
            axis_index_groups=self.row_groups,
        ).astype(jnp.float32)

    def row_sum(self, value):
        if self.wide:
            return value + self.to_core(value)
        return lax.psum(value, "mp", axis_index_groups=self.row_groups)


def shards(
    sizes,
    x_in,
    out_grad,
    item_lengths,
    weight_store,
    owner_perm,
    left_roots,
    right_roots,
    left_stats,
    right_stats,
    head_vectors,
    head_first,
    head_second,
    shared_vectors,
    shared_first,
    shared_second,
):
    batch_ways, model_ways = sizes
    shard_rows, model_width = x_in.shape
    fabric = Fabric(sizes, SLOTS // shard_rows)
    ways, panels, wide = fabric.ways, fabric.panels, fabric.wide
    dp_at, mp_at = lax.axis_index("dp"), lax.axis_index("mp")
    row_at, place_at = lax.div(mp_at, ways), lax.rem(mp_at, ways)

    owned, row_block, col_block = weight_store.shape[1:]
    head_part, shared_part = head_vectors.shape[1], shared_vectors.shape[0]
    head_count, shared_count = head_part * batch_ways, shared_part * batch_ways * model_ways
    block_count = owner_perm.shape[1]
    row_groups = model_width // row_block
    head_width = model_width // model_ways
    ffn_total = shared_count - 6 * model_width
    ffn_width = ffn_total // model_ways
    heads64, ffn64 = head_width // DH, ffn_width // DH
    hidden_rows = panels * (4 * head_width + 2 * ffn_width)
    panel_shape = (hidden_rows, model_width)
    half_a = (owned // 2) * DH + EXTRA
    blocks_a, blocks_b = owned // 2, owned - owned // 2

    def two_parts(value):
        high = lax.reduce_precision(value, 8, 7)
        return jnp.concatenate([high.astype(LOW), (value - high).astype(LOW)])

    blocks_low = jnp.swapaxes(weight_store[0], 1, 2).astype(LOW).reshape(owned * DH, 128)
    vectors = jnp.concatenate([two_parts(head_vectors[0]), two_parts(shared_vectors)])
    vectors = jnp.pad(vectors, (0, EXTRA * 128 - vectors.shape[0])).reshape(EXTRA, 128)
    own = jnp.concatenate(
        [blocks_low[: blocks_a * DH], vectors, blocks_low[blocks_a * DH :]], axis=0
    )

    if wide:
        perm_two = jnp.concatenate([owner_perm, fabric.to_x(owner_perm)], axis=0)
    else:
        perm_two = lax.all_gather(
            owner_perm, "mp", axis=0, tiled=True, axis_index_groups=fabric.same_groups
        )

    def place_of(perm, panel):
        col, row = lax.div(perm, row_groups), lax.rem(perm, row_groups)
        in_ffn = col - 4 * heads64
        at_head = lax.div(col, heads64) * panels * heads64 + panel * heads64 + lax.rem(col, heads64)
        at_ffn = (
            (4 * heads64 + lax.div(in_ffn, ffn64) * ffn64) * panels
            + panel * ffn64
            + lax.rem(in_ffn, ffn64)
        )
        return jnp.where(in_ffn < 0, at_head, at_ffn) * row_groups + row

    if wide:
        panel_ids = jnp.array([0, 1], jnp.int32)[:, None]
        panel_ids = lax.rem(panel_ids + row_at, 2)
    else:
        panel_ids = jnp.arange(panels, dtype=jnp.int32)[:, None]
    places = place_of(perm_two, panel_ids).reshape(panels, batch_ways, owned)

    if wide:
        rings = batch_ways // 2
        z_at, y_at = lax.div(dp_at, 2), lax.rem(dp_at, 2)
        step = jnp.arange(rings, dtype=jnp.int32)
        face = jnp.arange(2, dtype=jnp.int32)

        def owner_table(sign):
            z_of = lax.rem(z_at + sign * step + rings, rings)
            dp_of = z_of[:, None] * 2 + lax.rem(y_at + face, 2)[None, :]
            chosen = jnp.take(places, dp_of.reshape(-1), axis=1)
            chosen = chosen.reshape(2, rings, 2, owned).transpose(1, 2, 0, 3)
            return chosen.reshape(rings * 4, owned), dp_of

        table, dp_of = owner_table(-1)
        weights = None
        extras = []
        ring = own
        for k in range(rings):
            if k:
                ring = fabric.to_z(ring)
            by_x, by_y = fabric.to_x(ring), fabric.to_y(ring)
            far_a, far_b = fabric.to_x(by_y[:half_a]), fabric.to_y(by_x[half_a:])
            low_half, high_half = (0, 0, blocks_a), (half_a, blocks_a, blocks_b)

            def piece(entry, *halves):
                return [(row, entry, first, count) for row, first, count in halves]

            both = (low_half, high_half)
            weights = place(
                table,
                [ring, by_x, by_y, far_a, far_b],
                [
                    piece(4 * k, *both),
                    piece(4 * k + 1, *both),
                    piece(4 * k + 2, *both),
                    piece(4 * k + 3, low_half),
                    piece(4 * k + 3, (0, blocks_a, blocks_b)),
                ],
                panel_shape,
                weights,
            )
            cut = slice(blocks_a * DH, half_a)
            extras += [ring[cut], by_x[cut], by_y[cut], far_a[cut]]
        extras = jnp.stack(extras).reshape(rings, 2, 2, EXTRA, 128)
        extras = jnp.take(extras, lax.rem(z_at - step + rings, rings), axis=0)
        extras = jnp.take(extras, lax.rem(y_at + face, 2), axis=1)
        extras = jnp.take(extras, lax.rem(row_at + face, 2), axis=2)
        extras = extras.reshape(batch_ways, 2, EXTRA, 128)
    else:
        gathered = lax.all_gather(own, "mp", axis=0, axis_index_groups=fabric.same_groups)
        gathered = lax.all_gather(gathered, "dp", axis=0)
        table = places.transpose(1, 0, 2).reshape(batch_ways * panels, owned)
        extras = gathered[:, :, blocks_a * DH : half_a]
        stride = own.shape[0]
        flat = gathered.reshape(-1, 128)
        pieces = []
        for i in range(batch_ways * panels):
            pieces += [(i * stride, i, 0, blocks_a), (i * stride + half_a, i, blocks_a, blocks_b)]
        weights = place(table, [flat], [pieces], panel_shape)

    extras = extras.reshape(batch_ways, panels, EXTRA * 128).astype(jnp.float32)
    head_all = extras[:, :, :head_part] + extras[:, :, head_part : 2 * head_part]
    begin = 2 * head_part
    shared_all = (
        extras[:, :, begin : begin + shared_part]
        + extras[:, :, begin + shared_part : begin + 2 * shared_part]
    )
    head_all = head_all.transpose(1, 0, 2).reshape(panels, head_count)
    if wide:
        shared_other = fabric.to_core(shared_all)
        first = place_at == 0
        shared = jnp.stack(
            [
                jnp.where(first, shared_all, shared_other),
                jnp.where(first, shared_other, shared_all),
            ],
            axis=2,
        )
    else:
        shared = lax.all_gather(
            shared_all, "mp", axis=0, axis_index_groups=fabric.row_groups
        ).transpose(1, 2, 0, 3)
    shared = shared.reshape(shared_count)

    q_rows, f_rows = panels * head_width, panels * ffn_width
    w_qkv = weights[: 3 * q_rows]
    w_out = weights[3 * q_rows : 4 * q_rows]
    w_one = weights[4 * q_rows : 4 * q_rows + f_rows]
    w_two = weights[4 * q_rows + f_rows :]
    bias_query = head_all[:, :head_width].reshape(q_rows)
    bias_value = head_all[:, head_width:].reshape(q_rows)
    bias_qkv = jnp.concatenate([bias_query, jnp.zeros((q_rows,), jnp.float32), bias_value])
    scale_qkv = jnp.concatenate(
        [jnp.full((q_rows,), DH**-0.5, jnp.float32), jnp.ones((2 * q_rows,), jnp.float32)]
    )
    bias_output, bias_outer, gain_one, shift_one, gain_two, shift_two = (
        shared[i * model_width : (i + 1) * model_width] for i in range(6)
    )
    bias_inner = shared[6 * model_width :].reshape(panels, ways, ffn_width)
    bias_local = lax.dynamic_index_in_dim(bias_inner, place_at, 1, keepdims=False).reshape(f_rows)

    lengths = lax.dynamic_index_in_dim(item_lengths, row_at, 0, keepdims=False)
    starts = jnp.cumsum(lengths) - lengths

    x_row = fabric.row_gather(x_in)
    qkv = product(w_qkv, x_row, 1, 1) + bias_qkv[:, None]
    qkv = (qkv.astype(LOW) * scale_qkv[:, None].astype(LOW)).reshape(3, q_rows, SLOTS)
    context, log_total = attend(starts, lengths, qkv)
    attended = fabric.row_scatter(product(context, w_out, 0, 0))
    hidden = x_in.astype(jnp.float32) + attended + bias_output
    middle, middle_scaled, middle_inverse = normalize_keep(hidden, gain_one, shift_one)
    middle_row = fabric.row_gather(middle.astype(LOW))
    activated, slope = gelu_pair(product(middle_row, w_one, 1, 1) + bias_local)
    activated, slope = activated.astype(LOW), slope.astype(LOW)
    ffn_result = fabric.row_scatter(product(activated, w_two, 1, 0))
    outer_sum = middle + ffn_result + bias_outer
    layer_value, out_scaled, out_inverse = normalize_keep(outer_sum, gain_two, shift_two)

    resid_grad, grad_gain_two, grad_shift_two = normalize_back(
        out_grad.astype(jnp.float32), out_scaled, out_inverse, gain_two
    )
    grad_bias_outer = jnp.sum(resid_grad, axis=0)
    resid_row = fabric.row_gather(resid_grad.astype(LOW))
    before_grad = (product(resid_row, w_two, 1, 1) * slope.astype(jnp.float32)).astype(LOW)
    grad_w_two = product(activated, resid_row, 0, 0).astype(LOW)
    grad_w_one = product(before_grad, middle_row, 0, 0).astype(LOW)
    grad_bias_inner = jnp.sum(before_grad.astype(jnp.float32), axis=0)
    middle_grad = resid_grad + fabric.row_scatter(product(before_grad, w_one, 1, 0))
    hidden_grad, grad_gain_one, grad_shift_one = normalize_back(
        middle_grad, middle_scaled, middle_inverse, gain_one
    )
    grad_bias_output = jnp.sum(hidden_grad, axis=0)
    hidden_row = fabric.row_gather(hidden_grad.astype(LOW))
    grad_w_out = product(context, hidden_row, 1, 0).astype(LOW)
    dcontext = product(w_out, hidden_row, 1, 1).astype(LOW)
    qkv_grad = attend_back(starts, lengths, qkv, context, dcontext, log_total)
    qkv_grad = qkv_grad.reshape(3 * q_rows, SLOTS)
    grad_w_qkv = product(qkv_grad, x_row, 1, 0).astype(LOW)
    input_grad = hidden_grad + fabric.row_scatter(product(qkv_grad, w_qkv, 0, 0))
    column_sums = jnp.sum(qkv_grad.astype(jnp.float32), axis=1)

    head_grad = jnp.concatenate(
        [
            column_sums[:q_rows].reshape(panels, head_width),
            column_sums[2 * q_rows :].reshape(panels, head_width),
        ],
        axis=1,
    )
    inner_all = lax.dynamic_update_slice(
        jnp.zeros((panels, ways, ffn_width), jnp.float32),
        grad_bias_inner.reshape(panels, 1, ffn_width),
        (0, place_at, 0),
    )
    shared_grad = fabric.row_sum(
        jnp.concatenate(
            [
                grad_bias_output,
                grad_bias_outer,
                grad_gain_one,
                grad_shift_one,
                grad_gain_two,
                grad_shift_two,
                inner_all.reshape(ffn_total),
            ]
        )
    )
    shared_grad = shared_grad.reshape(batch_ways, panels, ways, shared_part)
    shared_grad = lax.dynamic_index_in_dim(shared_grad, place_at, 2, keepdims=False)
    head_grad = head_grad.reshape(panels, batch_ways, head_part).transpose(1, 0, 2)
    extra_grad = jnp.concatenate([head_grad, shared_grad], axis=2).astype(LOW)
    extra_grad = jnp.pad(
        extra_grad, ((0, 0), (0, 0), (0, EXTRA * 128 - head_part - shared_part))
    ).reshape(batch_ways, panels, EXTRA, 128)
    grads = jnp.concatenate([grad_w_qkv, grad_w_out, grad_w_one, grad_w_two], axis=0)

    if wide:
        table, dp_of = owner_table(1)
        extra_grad = jnp.take(extra_grad, dp_of.reshape(-1), axis=0)
        extra_grad = jnp.take(extra_grad, lax.rem(row_at + face, 2), axis=1)
        extra_grad = extra_grad.reshape(rings * 4, EXTRA, 128)
        running = None
        wide_type = jnp.float32
        for k in range(rings - 1, -1, -1):

            def low_of(entries):
                parts = []
                for i, entry in enumerate(entries):
                    parts.append((i * half_a, 4 * k + entry, 0, blocks_a))
                    parts.append((i * half_a + blocks_a * DH, 4 * k + entry, 0, 0))
                return parts

            def high_of(entries):
                return [
                    (i * blocks_b * DH, 4 * k + entry, blocks_a, blocks_b)
                    for i, entry in enumerate(entries)
                ]

            send_x, send_y, keep_a, keep_b = fetch(
                table,
                grads,
                extra_grad,
                [low_of((1, 3)), high_of((2, 3)), low_of((0, 2)), high_of((0, 1))],
            )
            got_x, got_y = fabric.to_x(send_x), fabric.to_y(send_y)
            half_b = blocks_b * DH
            sum_a = keep_a.astype(wide_type) + got_x.astype(wide_type)
            sum_b = keep_b.astype(wide_type) + got_y.astype(wide_type)
            far_a = fabric.to_y(sum_a[half_a:].astype(LOW))
            far_b = fabric.to_x(sum_b[half_b:].astype(LOW))
            here = jnp.concatenate(
                [
                    sum_a[:half_a] + far_a.astype(wide_type),
                    sum_b[:half_b] + far_b.astype(wide_type),
                ],
                axis=0,
            )
            if running is not None:
                here = here + running.astype(wide_type)
            if k:
                running = fabric.to_z(here.astype(LOW))
        reduced = here
    else:
        pieces = []
        for i in range(batch_ways * panels):
            base = i * own.shape[0]
            pieces += [
                (base, i, 0, blocks_a),
                (base + blocks_a * DH, i, 0, 0),
                (base + half_a, i, blocks_a, blocks_b),
            ]
        (chunks,) = fetch(
            table, grads, extra_grad.reshape(batch_ways * panels, EXTRA, 128), [pieces]
        )
        chunks = chunks.reshape(batch_ways, panels, own.shape[0], 128)
        chunks = lax.psum_scatter(chunks, "dp", scatter_dimension=0, tiled=False)
        reduced = lax.psum_scatter(
            chunks,
            "mp",
            scatter_dimension=0,
            tiled=False,
            axis_index_groups=fabric.same_groups,
        ).astype(jnp.float32)

    block_grads = jnp.concatenate([reduced[: blocks_a * DH], reduced[half_a:]], axis=0)
    block_grads = block_grads.reshape(owned, DH, 128)
    vector_grads = reduced[blocks_a * DH : half_a].reshape(EXTRA * 128)
    head_grad_mine = vector_grads[:head_part]
    shared_grad_mine = vector_grads[head_part : head_part + shared_part]

    precise = lax.Precision.HIGHEST
    weights_here = jnp.swapaxes(weight_store[0], 1, 2)
    token_total = shard_rows * model_ways * batch_ways
    scaled_grads = block_grads * token_total ** (-0.5)
    new_left = 0.5 * left_stats[0] + 0.5 * jnp.einsum(
        "bji,bjk->bik", scaled_grads, scaled_grads, precision=precise
    )
    new_right = 0.5 * right_stats[0] + 0.5 * jnp.einsum(
        "bij,bkj->bik", scaled_grads, scaled_grads, precision=precise
    )
    direction = jnp.einsum("bkj,bij->bki", block_grads, left_roots[0], precision=precise)
    direction = jnp.einsum("bkl,bki->bli", right_roots[0], direction, precision=precise)
    weight_size = jnp.sqrt(
        jnp.mean(weights_here * weights_here, axis=(1, 2), keepdims=True) + 1e-06
    )
    step_size = jnp.sqrt(jnp.mean(direction * direction, axis=(1, 2), keepdims=True) + 1e-06)
    new_weights = weights_here - 0.3 * weight_size * direction / step_size
    head_one, head_two, head_new = adam_update(
        head_vectors[0], head_first[0], head_second[0], head_grad_mine
    )
    shared_one, shared_two, shared_new = adam_update(
        shared_vectors, shared_first, shared_second, shared_grad_mine
    )
    return (
        layer_value.astype(LOW),
        input_grad,
        jnp.swapaxes(block_grads, 1, 2)[None],
        new_left[None],
        new_right[None],
        jnp.swapaxes(new_weights, 1, 2)[None],
        head_one[None],
        head_two[None],
        head_new[None],
        shared_one,
        shared_two,
        shared_new,
    )


def solution(mesh):
    rows, blocks, vector, head = P(BOTH, None), P("mp", "dp", None, None), P(BOTH), P("mp", "dp")
    return jax.shard_map(
        partial(shards, (mesh.shape["dp"], mesh.shape["mp"])),
        mesh=mesh,
        in_specs=(rows, rows, P("dp", None), blocks, P("mp", None))
        + (blocks,) * 4
        + (head,) * 3
        + (vector,) * 3,
        out_specs=(rows, rows) + (blocks,) * 4 + (head,) * 3 + (vector,) * 3,
        check_vma=False,
    )
```

time: 897 us -> 542 us (0.60)
  waiting for transfers between devices: 366 us -> 174 us
  blocking collectives: 128 us -> 0 us
  matrix products: 204 us -> 97.1 us
  Pallas kernels: 0 us -> 82.5 us
  starting transfers between devices: 0.41 us -> 43.8 us
  local copies, waits for them, and re-layouts: 95.3 us -> 54.4 us
  between operations: 16.5 us -> 2.24 us
  other arithmetic: 70.7 us -> 84 us
  loops' own time: 11.3 us -> 0 us
    all_gather x5 -> x0, waiting for transfers between devices: 187 us -> none  [the longest x1 76.5 us: shards(): lax.all_gather(weight_store, 'dp', axis=1, tiled=True)]
    reduce_scatter x5 -> x0, waiting for transfers between devices: 178 us -> none  [the longest x1 56.6 us: shards(): lax.psum_scatter(grad_owned.astype(jnp.bfloat16), 'dp', scatter_dimension...]
    ppermute x0 -> x49, waiting for transfers between devices: none -> 174 us  [send(): return lax.ppermute(value, BOTH, pairs)]
    unnamed x4 -> x0, blocking collectives: 128 us -> none
    dot_general x28 -> x14, matrix products: 193 us -> 86.2 us  [the longest x12 76.9 us: product(): lax.dot_general(left, right, (((left_dim,), (right_dim,)), ((), ())), pre...]
    pallas_call x0 -> x10, Pallas kernels: none -> 82.5 us  [the longest x1 22.4 us: attend_back(): pl.pallas_call(attend_back_kernel, out_shape=jax.ShapeDtypeStruct(qkv.sha...]
    ppermute x0 -> x49, starting transfers between devices: none -> 43.8 us  [send(): return lax.ppermute(value, BOTH, pairs)]
    concatenate x1 -> x5, other arithmetic: 0.01 us -> 34 us  [the longest x1 32.9 us: shards(): jnp.concatenate([grad_w_qkv, grad_w_out, grad_w_one, grad_w_two], axis=0)]
  transfers between devices with their start and end apart: 10 -> 49, of which waited for: 9 -> 23; matrix products, arithmetic and copies ran while one was open for 8% -> 12% of each run, Pallas kernels for 0% -> 5%
where the time goes in v1:
time: 542 us; the launch traced here: 538 us
  waiting for transfers between devices  174 us (32%)
  matrix products  97.1 us (18%)
  other arithmetic  84 us (15%)
  Pallas kernels  82.5 us (15%)
  local copies, waits for them, and re-layouts  54.4 us (10%)
  starting transfers between devices  43.8 us (8%)
    ppermute x49, waiting for transfers between devices, send(): return lax.ppermute(value, BOTH, pairs)  174 us
    dot_general x12, matrix products, product(): lax.dot_general(left, right, (((left_dim,), (right_dim,)), ((), ())), pre...  76.9 us
    ppermute x49, starting transfers between devices, send(): return lax.ppermute(value, BOTH, pairs)  43.8 us
    unnamed x161, local copies, waits for them, and re-layouts  33.4 us
    concatenate x1, other arithmetic, shards(): jnp.concatenate([grad_w_qkv, grad_w_out, grad_w_one, grad_w_two], axis=0)  32.9 us
    pallas_call x1, Pallas kernels, attend_back(): pl.pallas_call(attend_back_kernel, out_shape=jax.ShapeDtypeStruct(qkv.sha...  22.4 us
    pallas_call x4, Pallas kernels, place(): pl.pallas_call(partial(place_kernel, pieces, len(sources), shape[1] // 12...  20.6 us
    pallas_call x1, Pallas kernels, attend(): pl.pallas_call(attend_kernel, out_shape=(jax.ShapeDtypeStruct(qkv.shape[1...  20.4 us
  transfers between devices with their start and end apart: 49, of which 23 were waited for; matrix products, arithmetic and copies ran while one was open for 12% of the time, Pallas kernels for 5%

profile of v1, /device:TPU:0, one launch (start us, length us, event | category | flops | bytes accessed | tf_op | source)
XLA Modules:
  0.0 537.8 jit_solution(15924684164249300199)
XLA Ops:
  16.7 10.6 %collective-permute-done = s32[1,384]{1,0:T(1,128)S(1)} collective-permute-done((s32[1,384]{1,0:T(1,128)S(1)}, s32[1,384]{1,0:T(1,128)S(1)}, u32[]{:S(2)}, u32[]{:S(2)}) %collective-permute-start) | collective-permute-done | bytes 1568 | tf_op jit(solution)/shard_map/ppermute | solution.py:263
  43.9 5.8 %shard_map.247.refs_5_ = bf16[6144,1024]{1,0:T(8,128)(2,1)S(1)} custom-call(s32[16,48]{1,0:T(8,128)S(1)} %bitcast.219, bf16[3088,128]{1,0:T(8,128)(2,1)} %pad_maximum_fusion.14.refs_0_, bf16[3088,128]{1,0:T(8,128)(2,1)} %collective-permute-done.16.refs_1_, bf16[3088,128]{1,0:T(8,128)(2,1)} %collective-permute-done.17.refs_2_, ...), custom_call_target="tpu_custom_call" | custom-call | tf_op jit(solution)/shard_map/pallas_call | solution.py:193
  50.4 7.8 %collective-permute-done.13.refs_2_ = bf16[3088,128]{1,0:T(8,128)(2,1)S(1)} collective-permute-done((bf16[3088,128]{1,0:T(8,128)(2,1)}, bf16[3088,128]{1,0:T(8,128)(2,1)S(1)}, u32[]{:S(2)}, u32[]{:S(2)}) %collective-permute-start.13) | collective-permute-done | bytes 790560 | tf_op jit(solution)/shard_map/ppermute | solution.py:263
  64.3 6.7 %collective-permute-done.15.refs_4_ = bf16[1536,128]{1,0:T(8,128)(2,1)S(1)} collective-permute-done((bf16[1536,128]{1,0:T(8,128)(2,1)S(1)}, bf16[1536,128]{1,0:T(8,128)(2,1)S(1)}, u32[]{:S(2)}, u32[]{:S(2)}) %collective-permute-start.15) | collective-permute-done | bytes 393248 | tf_op jit(solution)/shard_map/ppermute | solution.py:263
  71.0 5.4 shard_map.248.refs_5_
  76.4 7.7 %collective-permute-done.9.refs_2_ = bf16[3088,128]{1,0:T(8,128)(2,1)S(1)} collective-permute-done((bf16[3088,128]{1,0:T(8,128)(2,1)S(1)}, bf16[3088,128]{1,0:T(8,128)(2,1)S(1)}, u32[]{:S(2)}, u32[]{:S(2)}) %collective-permute-start.9) | collective-permute-done | bytes 790560 | tf_op jit(solution)/shard_map/ppermute | solution.py:263
  88.5 10.0 %collective-permute-done.11.refs_4_ = bf16[1536,128]{1,0:T(8,128)(2,1)S(1)} collective-permute-done((bf16[1536,128]{1,0:T(8,128)(2,1)S(1)}, bf16[1536,128]{1,0:T(8,128)(2,1)S(1)}, u32[]{:S(2)}, u32[]{:S(2)}) %collective-permute-start.11) | collective-permute-done | bytes 393248 | tf_op jit(solution)/shard_map/ppermute | solution.py:263
  141.6 5.2 shard_map.250
  151.5 5.4 %fusion.7 = bf16[1536,1024]{1,0:T(8,128)(2,1)S(1)} fusion(f32[1536]{0:T(1024)S(1)} %pad_maximum_fusion.17, bf16[6144,1024]{1,0:T(8,128)(2,1)} %copy-done.3, bf16[1536]{0:T(1024)(128)(2,1)S(1)} %copy-done.64, bf16[512,1024]{1,0:T(8,128)(2,1)S(1)} %copy-done.38, bf16[512,1024]{1,0:T(8,128)(2,1)S(1)} %copy-done.37), kind=kOutput, calls=%fused_computation.24 | convolution fusion | flops 3230138368 | bytes 8397824 | tf_op jit(solution)/shard_map/dot_general | solution.py:41
  156.9 20.4 %shard_map.251 = (bf16[512,1024]{1,0:T(8,128)(2,1)S(1)}, f32[8,1,1024]{2,1,0:T(1,128)S(1)}) custom-call(s32[8]{0:T(128)S(1)} %get-tuple-element.71.start_ref, s32[8]{0:T(128)S(1)} %copy-done.14, bf16[3,512,1024]{2,1,0:T(8,128)(2,1)S(1)} %bitcast.227), custom_call_target="tpu_custom_call" | custom-call | flops 4294967296 | bytes 4194304 | tf_op jit(solution)/shard_map/pallas_call | solution.py:121
  195.6 9.7 %multiply_convert_fusion.1 = (bf16[1024,2048]{1,0:T(8,128)(2,1)S(1)}, f32[1024,2048]{1,0:T(8,128)}) fusion(f32[2048]{0:T(1024)S(1)} %bitcast.244, bf16[6144,1024]{1,0:T(8,128)(2,1)} %copy-done.3, bf16[512,1024]{1,0:T(8,128)(2,1)S(1)} %get-tuple-element.79, bf16[512,1024]{1,0:T(8,128)(2,1)S(1)} %get-tuple-element.78), kind=kOutput, calls=%fused_computation.11 | convolution fusion | flops 4311744512 | bytes 18882560 | tf_op jit(solution)/shard_map/dot_general | solution.py:41
  205.3 7.8 %fusion.1 = f32[1024,1024]{1,0:T(8,128)S(1)} fusion(bf16[1024,2048]{1,0:T(8,128)(2,1)S(1)} %get-tuple-element.105, bf16[6144,1024]{1,0:T(8,128)(2,1)} %copy-done.3), kind=kOutput, calls=%fused_computation.18 | convolution fusion | flops 4294967296 | bytes 12582912 | tf_op jit(solution)/shard_map/dot_general | solution.py:41
  228.5 10.9 %convert_reduce_fusion = (f32[2048]{0:T(1024)S(1)}, bf16[1024,2048]{1,0:T(8,128)(2,1)S(1)}) fusion(f32[1024,2048]{1,0:T(8,128)} %get-tuple-element.106, f32[2048]{0:T(1024)S(1)} %bitcast.245, bf16[6144,1024]{1,0:T(8,128)(2,1)} %copy-done.3, bf16[512,1024]{1,0:T(8,128)(2,1)S(1)} %get-tuple-element.77, bf16[512,1024]{1,0:T(8,128)(2,1)S(1)} %get-tuple-element.76), kind=kOutput, calls=%fused_computation.8 | convolution fusion | flops 4330616832 | bytes 18890752 | tf_op jit(solution)/shard_map/dot_general | solution.py:41
  239.5 7.8 %fusion.3 = f32[1024,1024]{1,0:T(8,128)S(1)} fusion(bf16[1024,2048]{1,0:T(8,128)(2,1)S(1)} %get-tuple-element.108, bf16[6144,1024]{1,0:T(8,128)(2,1)} %copy-done.3), kind=kOutput, calls=%fused_computation.20 | convolution fusion | flops 4294967296 | bytes 12582912 | tf_op jit(solution)/shard_map/dot_general | solution.py:41
  250.4 9.5 %convolution_convert_fusion.2 = bf16[2048,1024]{1,0:T(8,128)(2,1)} fusion(bf16[1024,2048]{1,0:T(8,128)(2,1)} %copy-done.67, bf16[512,1024]{1,0:T(8,128)(2,1)} %copy-done.41, bf16[512,1024]{1,0:T(8,128)(2,1)} %copy-done.40), kind=kOutput, calls=%fused_computation.16 | convolution fusion | flops 4301258752 | bytes 10485760 | tf_op jit(solution)/shard_map/dot_general | solution.py:41
  266.2 6.5 %convolution_convert_fusion.1 = bf16[2048,1024]{1,0:T(8,128)(2,1)} fusion(bf16[1024,2048]{1,0:T(8,128)(2,1)S(1)} %copy-done.66, bf16[512,1024]{1,0:T(8,128)(2,1)S(1)} %copy-done.45, bf16[512,1024]{1,0:T(8,128)(2,1)S(1)} %copy-done.43), kind=kOutput, calls=%fused_computation.15 | convolution fusion | flops 4301258752 | bytes 10485760 | tf_op jit(solution)/shard_map/dot_general | solution.py:41
  279.9 22.4 %shard_map.252 = bf16[3,512,1024]{2,1,0:T(8,128)(2,1)S(1)} custom-call(s32[8]{0:T(128)S(1)} %get-tuple-element.71.start_ref, s32[8]{0:T(128)S(1)} %copy-done.14, bf16[3,512,1024]{2,1,0:T(8,128)(2,1)S(1)} %bitcast.228, bf16[512,1024]{1,0:T(8,128)(2,1)S(1)} %copy-done.11, bf16[512,1024]{1,0:T(8,128)(2,1)S(1)} %convolution_convert_fusion.4.dctx_ref, ...), custom_call_target="tpu_custom_call" | custom-call | flops 10737418240 | bytes 8388608 | tf_op jit(solution)/shard_map/pallas_call | solution.py:147
  308.1 6.1 %convolution_convert_fusion = bf16[1536,1024]{1,0:T(8,128)(2,1)S(1)} fusion(bf16[1536,1024]{1,0:T(8,128)(2,1)} %bitcast.217, bf16[512,1024]{1,0:T(8,128)(2,1)} %get-tuple-element.81, bf16[512,1024]{1,0:T(8,128)(2,1)} %get-tuple-element.80), kind=kOutput, calls=%fused_computation.14 | convolution fusion | flops 3226992640 | bytes 8388608 | tf_op jit(solution)/shard_map/dot_general | solution.py:41
  314.3 32.9 %pad_maximum_fusion.grad_ref = bf16[6144,1024]{1,0:T(8,128)(2,1)S(1)} fusion(bf16[2048,1024]{1,0:T(8,128)(2,1)S(1)} %copy-done.29, bf16[2048,1024]{1,0:T(8,128)(2,1)S(1)} %copy-done.28, bf16[512,1024]{1,0:T(8,128)(2,1)S(1)} %copy-done.39, bf16[1536,1024]{1,0:T(8,128)(2,1)S(1)} %convolution_convert_fusion), kind=kLoop, calls=%fused_computation.7 | loop fusion | flops 50331648 | bytes 25165824 | tf_op jit(solution)/shard_map/concatenate | solution.py:555
  347.2 4.8 shard_map.256
  356.8 6.6 %collective-permute-start.42 = (bf16[3104,128]{1,0:T(8,128)(2,1)S(1)}, bf16[3104,128]{1,0:T(8,128)(2,1)S(1)}, u32[]{:S(2)}, u32[]{:S(2)}) collective-permute-start(bf16[3104,128]{1,0:T(8,128)(2,1)S(1)} %get-tuple-element.46), channel_id=1, source_target_pairs={{0,2},{1,3},{2,0},{3,1},{4,6},{5,7},{6,4},{7,5},{8,10},{9,11},{10,... | collective-permute-start | bytes 2383880 | tf_op jit(solution)/shard_map/ppermute | solution.py:263
  365.5 5.5 %fusion.15 = f32[1024,1024]{1,0:T(8,128)S(1)} fusion(bf16[1536,1024]{1,0:T(8,128)(2,1)S(1)} %bitcast.218, bf16[6144,1024]{1,0:T(8,128)(2,1)} %copy-done.3), kind=kOutput, calls=%fused_computation.36 | convolution fusion | flops 3221225472 | bytes 10485760 | tf_op jit(solution)/shard_map/dot_general | solution.py:41
  386.0 14.7 %collective-permute-done.40 = bf16[3072,128]{1,0:T(8,128)(2,1)} collective-permute-done((bf16[3072,128]{1,0:T(8,128)(2,1)S(1)}, bf16[3072,128]{1,0:T(8,128)(2,1)}, u32[]{:S(2)}, u32[]{:S(2)}) %collective-permute-start.40) | collective-permute-done | bytes 786464 | tf_op jit(solution)/shard_map/ppermute | solution.py:263
  402.1 15.4 %collective-permute-done.36 = bf16[3072,128]{1,0:T(8,128)(2,1)S(1)} collective-permute-done((bf16[3072,128]{1,0:T(8,128)(2,1)S(1)}, bf16[3072,128]{1,0:T(8,128)(2,1)S(1)}, u32[]{:S(2)}, u32[]{:S(2)}) %collective-permute-start.36) | collective-permute-done | bytes 786464 | tf_op jit(solution)/shard_map/ppermute | solution.py:263
  417.9 15.5 %collective-permute-done.32 = bf16[3072,128]{1,0:T(8,128)(2,1)S(1)} collective-permute-done((bf16[3072,128]{1,0:T(8,128)(2,1)S(1)}, bf16[3072,128]{1,0:T(8,128)(2,1)S(1)}, u32[]{:S(2)}, u32[]{:S(2)}) %collective-permute-start.32) | collective-permute-done | bytes 786464 | tf_op jit(solution)/shard_map/ppermute | solution.py:263
  445.9 5.1 collective-permute-done.43
  454.4 5.1 collective-permute-done.39
  459.8 14.8 %collective-permute-done.46 = bf16[3088,128]{1,0:T(8,128)(2,1)S(1)} collective-permute-done((bf16[3088,128]{1,0:T(8,128)(2,1)S(1)}, bf16[3088,128]{1,0:T(8,128)(2,1)S(1)}, u32[]{:S(2)}, u32[]{:S(2)}) %collective-permute-start.46) | collective-permute-done | bytes 790560 | tf_op jit(solution)/shard_map/ppermute | solution.py:263
  475.1 19.6 %collective-permute-done.47 = bf16[3088,128]{1,0:T(8,128)(2,1)S(1)} collective-permute-done((bf16[3088,128]{1,0:T(8,128)(2,1)S(1)}, bf16[3088,128]{1,0:T(8,128)(2,1)S(1)}, u32[]{:S(2)}, u32[]{:S(2)}) %collective-permute-start.47) | collective-permute-done | bytes 790560 | tf_op jit(solution)/shard_map/ppermute | solution.py:263
  495.6 18.7 %collective-permute-done.48 = bf16[3088,128]{1,0:T(8,128)(2,1)S(1)} collective-permute-done((bf16[3088,128]{1,0:T(8,128)(2,1)S(1)}, bf16[3088,128]{1,0:T(8,128)(2,1)S(1)}, u32[]{:S(2)}, u32[]{:S(2)}) %collective-permute-start.48) | collective-permute-done | bytes 790560 | tf_op jit(solution)/shard_map/ppermute | solution.py:263
  514.7 6.2 %fusion.8 = f32[48,64,128]{2,1,0:T(8,128)S(1)} fusion(f32[48,64,128]{2,1,0:T(8,128)S(1)} %bitcast.229, f32[1,48,128,128]{3,2,1,0:T(8,128)S(1)} %copy-done), kind=kOutput, calls=%fused_computation.25 | convolution fusion | flops 603979776 | bytes 6291456 | tf_op jit(solution)/shard_map/bkj,bij->bki/dot_general | solution.py:641
  524.1 7.0 %fusion.11 = f32[1,48,128,128]{3,2,1,0:T(8,128)} fusion(f32[1,48,128,128]{3,2,1,0:T(8,128)S(1)} %copy-done.30, f32[48,64,128]{2,1,0:T(8,128)S(1)} %bitcast.230), kind=kOutput, calls=%fused_computation.29 | convolution fusion | flops 605945856 | bytes 7864320 | tf_op jit(solution)/shard_map/bji,bjk->bik/dot_general | solution.py:635
  (410 shorter events, 198.1 us)
Async XLA Ops:
  4.9 23.3 %collective-permute-start.17 = (bf16[3088,128]{1,0:T(8,128)(2,1)}, bf16[3088,128]{1,0:T(8,128)(2,1)}, u32[]{:S(2)}, u32[]{:S(2)}) collective-permute-start(bf16[3088,128]{1,0:T(8,128)(2,1)} %pad_maximum_fusion.14.refs_0_), channel_id=1, source_target_pairs={{0,4},{1,5},{2,6},{3,7},{4,0},{5,1},{6,2},{7,3},{8,12},{9,13},{10,... | collective-permute-start | bytes 2371592 | tf_op jit(solution)/shard_map/ppermute | solution.py:263
  7.9 22.9 %collective-permute-start.16 = (bf16[3088,128]{1,0:T(8,128)(2,1)}, bf16[3088,128]{1,0:T(8,128)(2,1)}, u32[]{:S(2)}, u32[]{:S(2)}) collective-permute-start(bf16[3088,128]{1,0:T(8,128)(2,1)} %pad_maximum_fusion.14.refs_0_), channel_id=1, source_target_pairs={{0,2},{1,3},{2,0},{3,1},{4,6},{5,7},{6,4},{7,5},{8,10},{9,11},{10,... | collective-permute-start | bytes 2371592 | tf_op jit(solution)/shard_map/ppermute | solution.py:263
  9.4 23.0 %collective-permute-start.1 = (bf16[3088,128]{1,0:T(8,128)(2,1)}, bf16[3088,128]{1,0:T(8,128)(2,1)}, u32[]{:S(2)}, u32[]{:S(2)}) collective-permute-start(bf16[3088,128]{1,0:T(8,128)(2,1)} %pad_maximum_fusion.14.refs_0_), channel_id=1, source_target_pairs={{0,8},{1,9},{2,10},{3,11},{4,12},{5,13},{6,14},{7,15},{8,16},{9,17... | collective-permute-start | bytes 2371592 | tf_op jit(solution)/shard_map/ppermute | solution.py:263
  11.0 16.4 %collective-permute-start = (s32[1,384]{1,0:T(1,128)S(1)}, s32[1,384]{1,0:T(1,128)S(1)}, u32[]{:S(2)}, u32[]{:S(2)}) collective-permute-start(s32[1,384]{1,0:T(1,128)S(1)} %copy-done.59), channel_id=1, source_target_pairs={{0,2},{1,3},{2,0},{3,1},{4,6},{5,7},{6,4},{7,5},{8,10},{9,11},{10,... | collective-permute-start | bytes 4616 | tf_op jit(solution)/shard_map/ppermute | solution.py:263
  11.5 23.6 %collective-permute-start.20 = (bf16[512,1024]{1,0:T(8,128)(2,1)}, bf16[512,1024]{1,0:T(8,128)(2,1)}, u32[]{:S(2)}, u32[]{:S(2)}) collective-permute-start(bf16[512,1024]{1,0:T(8,128)(2,1)} %param.18), channel_id=1, source_target_pairs={{0,1},{1,0},{2,3},{3,2},{4,5},{5,4},{6,7},{7,6},{8,9},{9,8},{10,11... | collective-permute-start | bytes 3145736 | tf_op jit(solution)/shard_map/ppermute | solution.py:263
  29.2 14.7 %collective-permute-start.18 = (bf16[1552,128]{1,0:T(8,128)(2,1)S(1)}, bf16[1552,128]{1,0:T(8,128)(2,1)S(1)}, u32[]{:S(2)}, u32[]{:S(2)}) collective-permute-start(bf16[1552,128]{1,0:T(8,128)(2,1)S(1)} %slice.308), channel_id=1, source_target_pairs={{0,2},{1,3},{2,0},{3,1},{4,6},{5,7},{6,4},{7,5},{8,10},{9,11},{10,... | collective-permute-start | bytes 1191944 | tf_op jit(solution)/shard_map/ppermute | solution.py:263
  32.4 25.8 %collective-permute-start.13 = (bf16[3088,128]{1,0:T(8,128)(2,1)}, bf16[3088,128]{1,0:T(8,128)(2,1)S(1)}, u32[]{:S(2)}, u32[]{:S(2)}) collective-permute-start(bf16[3088,128]{1,0:T(8,128)(2,1)} %collective-permute-done.1.refs_0_), channel_id=1, source_target_pairs={{0,4},{1,5},{2,6},{3,7},{4,0},{5,1},{6,2},{7,3},{8,12},{9,13},{10,... | collective-permute-start | bytes 2371592 | tf_op jit(solution)/shard_map/ppermute | solution.py:263
  33.9 24.9 %collective-permute-start.12 = (bf16[3088,128]{1,0:T(8,128)(2,1)}, bf16[3088,128]{1,0:T(8,128)(2,1)S(1)}, u32[]{:S(2)}, u32[]{:S(2)}) collective-permute-start(bf16[3088,128]{1,0:T(8,128)(2,1)} %collective-permute-done.1.refs_0_), channel_id=1, source_target_pairs={{0,2},{1,3},{2,0},{3,1},{4,6},{5,7},{6,4},{7,5},{8,10},{9,11},{10,... | collective-permute-start | bytes 2371592 | tf_op jit(solution)/shard_map/ppermute | solution.py:263
  35.1 24.4 %collective-permute-start.2 = (bf16[3088,128]{1,0:T(8,128)(2,1)}, bf16[3088,128]{1,0:T(8,128)(2,1)S(1)}, u32[]{:S(2)}, u32[]{:S(2)}) collective-permute-start(bf16[3088,128]{1,0:T(8,128)(2,1)} %collective-permute-done.1.refs_0_), channel_id=1, source_target_pairs={{0,8},{1,9},{2,10},{3,11},{4,12},{5,13},{6,14},{7,15},{8,16},{9,17... | collective-permute-start | bytes 2371592 | tf_op jit(solution)/shard_map/ppermute | solution.py:263
  59.5 24.5 %collective-permute-start.9 = (bf16[3088,128]{1,0:T(8,128)(2,1)S(1)}, bf16[3088,128]{1,0:T(8,128)(2,1)S(1)}, u32[]{:S(2)}, u32[]{:S(2)}) collective-permute-start(bf16[3088,128]{1,0:T(8,128)(2,1)S(1)} %collective-permute-done.2.refs_0_), channel_id=1, source_target_pairs={{0,4},{1,5},{2,6},{3,7},{4,0},{5,1},{6,2},{7,3},{8,12},{9,13},{10,... | collective-permute-start | bytes 2371592 | tf_op jit(solution)/shard_map/ppermute | solution.py:263
  61.0 25.3 %collective-permute-start.8 = (bf16[3088,128]{1,0:T(8,128)(2,1)S(1)}, bf16[3088,128]{1,0:T(8,128)(2,1)S(1)}, u32[]{:S(2)}, u32[]{:S(2)}) collective-permute-start(bf16[3088,128]{1,0:T(8,128)(2,1)S(1)} %collective-permute-done.2.refs_0_), channel_id=1, source_target_pairs={{0,2},{1,3},{2,0},{3,1},{4,6},{5,7},{6,4},{7,5},{8,10},{9,11},{10,... | collective-permute-start | bytes 2371592 | tf_op jit(solution)/shard_map/ppermute | solution.py:263
  62.5 24.0 %collective-permute-start.3 = (bf16[3088,128]{1,0:T(8,128)(2,1)S(1)}, bf16[3088,128]{1,0:T(8,128)(2,1)S(1)}, u32[]{:S(2)}, u32[]{:S(2)}) collective-permute-start(bf16[3088,128]{1,0:T(8,128)(2,1)S(1)} %collective-permute-done.2.refs_0_), channel_id=1, source_target_pairs={{0,8},{1,9},{2,10},{3,11},{4,12},{5,13},{6,14},{7,15},{8,16},{9,17... | collective-permute-start | bytes 2371592 | tf_op jit(solution)/shard_map/ppermute | solution.py:263
  84.1 14.3 %collective-permute-start.10 = (bf16[1552,128]{1,0:T(8,128)(2,1)S(1)}, bf16[1552,128]{1,0:T(8,128)(2,1)S(1)}, u32[]{:S(2)}, u32[]{:S(2)}) collective-permute-start(bf16[1552,128]{1,0:T(8,128)(2,1)S(1)} %slice.304), channel_id=1, source_target_pairs={{0,2},{1,3},{2,0},{3,1},{4,6},{5,7},{6,4},{7,5},{8,10},{9,11},{10,... | collective-permute-start | bytes 1191944 | tf_op jit(solution)/shard_map/ppermute | solution.py:263
  86.4 23.3 %collective-permute-start.5 = (bf16[3088,128]{1,0:T(8,128)(2,1)S(1)}, bf16[3088,128]{1,0:T(8,128)(2,1)S(1)}, u32[]{:S(2)}, u32[]{:S(2)}) collective-permute-start(bf16[3088,128]{1,0:T(8,128)(2,1)S(1)} %collective-permute-done.3.refs_0_), channel_id=1, source_target_pairs={{0,4},{1,5},{2,6},{3,7},{4,0},{5,1},{6,2},{7,3},{8,12},{9,13},{10,... | collective-permute-start | bytes 2371592 | tf_op jit(solution)/shard_map/ppermute | solution.py:263
  88.4 23.0 %collective-permute-start.4 = (bf16[3088,128]{1,0:T(8,128)(2,1)S(1)}, bf16[3088,128]{1,0:T(8,128)(2,1)S(1)}, u32[]{:S(2)}, u32[]{:S(2)}) collective-permute-start(bf16[3088,128]{1,0:T(8,128)(2,1)S(1)} %collective-permute-done.3.refs_0_), channel_id=1, source_target_pairs={{0,2},{1,3},{2,0},{3,1},{4,6},{5,7},{6,4},{7,5},{8,10},{9,11},{10,... | collective-permute-start | bytes 2371592 | tf_op jit(solution)/shard_map/ppermute | solution.py:263
  112.3 21.3 %collective-permute-start.7 = (bf16[1536,128]{1,0:T(8,128)(2,1)}, bf16[1536,128]{1,0:T(8,128)(2,1)}, u32[]{:S(2)}, u32[]{:S(2)}) collective-permute-start(bf16[1536,128]{1,0:T(8,128)(2,1)} %slice.303), channel_id=1, source_target_pairs={{0,4},{1,5},{2,6},{3,7},{4,0},{5,1},{6,2},{7,3},{8,12},{9,13},{10,... | collective-permute-start | bytes 1179656 | tf_op jit(solution)/shard_map/ppermute | solution.py:263
  356.8 76.7 %collective-permute-start.42 = (bf16[3104,128]{1,0:T(8,128)(2,1)S(1)}, bf16[3104,128]{1,0:T(8,128)(2,1)S(1)}, u32[]{:S(2)}, u32[]{:S(2)}) collective-permute-start(bf16[3104,128]{1,0:T(8,128)(2,1)S(1)} %get-tuple-element.46), channel_id=1, source_target_pairs={{0,2},{1,3},{2,0},{3,1},{4,6},{5,7},{6,4},{7,5},{8,10},{9,11},{10,... | collective-permute-start | bytes 2383880 | tf_op jit(solution)/shard_map/ppermute | solution.py:263
  363.4 21.3 %collective-permute-start.44 = (bf16[3072,128]{1,0:T(8,128)(2,1)S(1)}, bf16[3072,128]{1,0:T(8,128)(2,1)}, u32[]{:S(2)}, u32[]{:S(2)}) collective-permute-start(bf16[3072,128]{1,0:T(8,128)(2,1)S(1)} %get-tuple-element.48), channel_id=1, source_target_pairs={{0,4},{1,5},{2,6},{3,7},{4,0},{5,1},{6,2},{7,3},{8,12},{9,13},{10,... | collective-permute-start | bytes 2359304 | tf_op jit(solution)/shard_map/ppermute | solution.py:263
  363.4 70.7 %collective-permute-start.38 = (bf16[3104,128]{1,0:T(8,128)(2,1)S(1)}, bf16[3104,128]{1,0:T(8,128)(2,1)S(1)}, u32[]{:S(2)}, u32[]{:S(2)}) collective-permute-start(bf16[3104,128]{1,0:T(8,128)(2,1)S(1)} %get-tuple-element.42), channel_id=1, source_target_pairs={{0,2},{1,3},{2,0},{3,1},{4,6},{5,7},{6,4},{7,5},{8,10},{9,11},{10,... | collective-permute-start | bytes 2383880 | tf_op jit(solution)/shard_map/ppermute | solution.py:263
  363.5 37.2 %collective-permute-start.40 = (bf16[3072,128]{1,0:T(8,128)(2,1)S(1)}, bf16[3072,128]{1,0:T(8,128)(2,1)}, u32[]{:S(2)}, u32[]{:S(2)}) collective-permute-start(bf16[3072,128]{1,0:T(8,128)(2,1)S(1)} %get-tuple-element.44), channel_id=1, source_target_pairs={{0,4},{1,5},{2,6},{3,7},{4,0},{5,1},{6,2},{7,3},{8,12},{9,13},{10,... | collective-permute-start | bytes 2359304 | tf_op jit(solution)/shard_map/ppermute | solution.py:263
  382.7 53.3 %collective-permute-start.34 = (bf16[3104,128]{1,0:T(8,128)(2,1)S(1)}, bf16[3104,128]{1,0:T(8,128)(2,1)S(1)}, u32[]{:S(2)}, u32[]{:S(2)}) collective-permute-start(bf16[3104,128]{1,0:T(8,128)(2,1)S(1)} %get-tuple-element.38), channel_id=1, source_target_pairs={{0,2},{1,3},{2,0},{3,1},{4,6},{5,7},{6,4},{7,5},{8,10},{9,11},{10,... | collective-permute-start | bytes 2383880 | tf_op jit(solution)/shard_map/ppermute | solution.py:263
  384.7 32.8 %collective-permute-start.36 = (bf16[3072,128]{1,0:T(8,128)(2,1)S(1)}, bf16[3072,128]{1,0:T(8,128)(2,1)S(1)}, u32[]{:S(2)}, u32[]{:S(2)}) collective-permute-start(bf16[3072,128]{1,0:T(8,128)(2,1)S(1)} %get-tuple-element.40), channel_id=1, source_target_pairs={{0,4},{1,5},{2,6},{3,7},{4,0},{5,1},{6,2},{7,3},{8,12},{9,13},{10,... | collective-permute-start | bytes 2359304 | tf_op jit(solution)/shard_map/ppermute | solution.py:263
  400.8 32.5 %collective-permute-start.32 = (bf16[3072,128]{1,0:T(8,128)(2,1)S(1)}, bf16[3072,128]{1,0:T(8,128)(2,1)S(1)}, u32[]{:S(2)}, u32[]{:S(2)}) collective-permute-start(bf16[3072,128]{1,0:T(8,128)(2,1)S(1)} %get-tuple-element.36), channel_id=1, source_target_pairs={{0,4},{1,5},{2,6},{3,7},{4,0},{5,1},{6,2},{7,3},{8,12},{9,13},{10,... | collective-permute-start | bytes 2359304 | tf_op jit(solution)/shard_map/ppermute | solution.py:263
  417.5 19.1 %collective-permute-start.30 = (bf16[3104,128]{1,0:T(8,128)(2,1)S(1)}, bf16[3104,128]{1,0:T(8,128)(2,1)S(1)}, u32[]{:S(2)}, u32[]{:S(2)}) collective-permute-start(bf16[3104,128]{1,0:T(8,128)(2,1)S(1)} %get-tuple-element.34), channel_id=1, source_target_pairs={{0,2},{1,3},{2,0},{3,1},{4,6},{5,7},{6,4},{7,5},{8,10},{9,11},{10,... | collective-permute-start | bytes 2383880 | tf_op jit(solution)/shard_map/ppermute | solution.py:263
  434.1 19.8 %collective-permute-start.41 = (bf16[1536,128]{1,0:T(8,128)(2,1)S(1)}, bf16[1536,128]{1,0:T(8,128)(2,1)S(1)}, u32[]{:S(2)}, u32[]{:S(2)}) collective-permute-start(bf16[1536,128]{1,0:T(8,128)(2,1)S(1)} %slice.474), channel_id=1, source_target_pairs={{0,2},{1,3},{2,0},{3,1},{4,6},{5,7},{6,4},{7,5},{8,10},{9,11},{10,... | collective-permute-start | bytes 1179656 | tf_op jit(solution)/shard_map/ppermute | solution.py:263
  436.0 38.9 %collective-permute-start.37 = (bf16[1536,128]{1,0:T(8,128)(2,1)S(1)}, bf16[1536,128]{1,0:T(8,128)(2,1)S(1)}, u32[]{:S(2)}, u32[]{:S(2)}) collective-permute-start(bf16[1536,128]{1,0:T(8,128)(2,1)S(1)} %slice.475), channel_id=1, source_target_pairs={{0,2},{1,3},{2,0},{3,1},{4,6},{5,7},{6,4},{7,5},{8,10},{9,11},{10,... | collective-permute-start | bytes 1179656 | tf_op jit(solution)/shard_map/ppermute | solution.py:263
  436.6 58.8 %collective-permute-start.33 = (bf16[1536,128]{1,0:T(8,128)(2,1)S(1)}, bf16[1536,128]{1,0:T(8,128)(2,1)S(1)}, u32[]{:S(2)}, u32[]{:S(2)}) collective-permute-start(bf16[1536,128]{1,0:T(8,128)(2,1)S(1)} %slice.476), channel_id=1, source_target_pairs={{0,2},{1,3},{2,0},{3,1},{4,6},{5,7},{6,4},{7,5},{8,10},{9,11},{10,... | collective-permute-start | bytes 1179656 | tf_op jit(solution)/shard_map/ppermute | solution.py:263
  450.9 24.1 %collective-permute-start.35 = (bf16[1552,128]{1,0:T(8,128)(2,1)S(1)}, bf16[1552,128]{1,0:T(8,128)(2,1)S(1)}, u32[]{:S(2)}, u32[]{:S(2)}) collective-permute-start(bf16[1552,128]{1,0:T(8,128)(2,1)S(1)} %slice.471), channel_id=1, source_target_pairs={{0,4},{1,5},{2,6},{3,7},{4,0},{5,1},{6,2},{7,3},{8,12},{9,13},{10,... | collective-permute-start | bytes 1191944 | tf_op jit(solution)/shard_map/ppermute | solution.py:263
  453.9 20.7 %collective-permute-start.46 = (bf16[3088,128]{1,0:T(8,128)(2,1)S(1)}, bf16[3088,128]{1,0:T(8,128)(2,1)S(1)}, u32[]{:S(2)}, u32[]{:S(2)}) collective-permute-start(bf16[3088,128]{1,0:T(8,128)(2,1)S(1)} %pad_maximum_fusion.15), channel_id=1, source_target_pairs={{0,8},{1,9},{2,10},{3,11},{4,12},{5,13},{6,14},{7,15},{8,16},{9,17... | collective-permute-start | bytes 2371592 | tf_op jit(solution)/shard_map/ppermute | solution.py:263
  459.5 36.0 %collective-permute-start.31 = (bf16[1552,128]{1,0:T(8,128)(2,1)S(1)}, bf16[1552,128]{1,0:T(8,128)(2,1)S(1)}, u32[]{:S(2)}, u32[]{:S(2)}) collective-permute-start(bf16[1552,128]{1,0:T(8,128)(2,1)S(1)} %slice.472), channel_id=1, source_target_pairs={{0,4},{1,5},{2,6},{3,7},{4,0},{5,1},{6,2},{7,3},{8,12},{9,13},{10,... | collective-permute-start | bytes 1191944 | tf_op jit(solution)/shard_map/ppermute | solution.py:263
  474.9 19.9 %collective-permute-start.47 = (bf16[3088,128]{1,0:T(8,128)(2,1)S(1)}, bf16[3088,128]{1,0:T(8,128)(2,1)S(1)}, u32[]{:S(2)}, u32[]{:S(2)}) collective-permute-start(bf16[3088,128]{1,0:T(8,128)(2,1)S(1)} %fusion.24), channel_id=1, source_target_pairs={{0,8},{1,9},{2,10},{3,11},{4,12},{5,13},{6,14},{7,15},{8,16},{9,17... | collective-permute-start | bytes 2371592 | tf_op jit(solution)/shard_map/ppermute | solution.py:263
  494.9 19.3 %collective-permute-start.48 = (bf16[3088,128]{1,0:T(8,128)(2,1)S(1)}, bf16[3088,128]{1,0:T(8,128)(2,1)S(1)}, u32[]{:S(2)}, u32[]{:S(2)}) collective-permute-start(bf16[3088,128]{1,0:T(8,128)(2,1)S(1)} %fusion.23), channel_id=1, source_target_pairs={{0,8},{1,9},{2,10},{3,11},{4,12},{5,13},{6,14},{7,15},{8,16},{9,17... | collective-permute-start | bytes 2371592 | tf_op jit(solution)/shard_map/ppermute | solution.py:263
  (85 other events, 1014.0 us)
